TPU v7x, 32 devices: a whole 2x2x4 slice. The times are simulated.
32 devices in a mesh: group: 8 (over z, y), inner: 4 (over x, core).
Axes of the slice: x: 2, y: 2, z: 4, core: 2. Of those that a mesh axis runs over, the one named last changes fastest.
Arguments:
- tokens: bfloat16 [1024, 7168], P('group', 'inner'), may hold values from -6 to 6
- routes: int32 [1024, 4], P('group'), may hold values from 0 to 7, all different within a row; in each aligned block of 128 rows (0 to 127, 128 to 255, ...) at most 96 rows name the same one
- gate_weights: float32 [1024, 4], P('group'), may hold values from 0.1 to 1
- w_gate: bfloat16 [8, 7168, 2048], P('group', None, 'inner'), may hold values from -0.0625 to 0.0625
- w_up: bfloat16 [8, 7168, 2048], P('group', None, 'inner'), may hold values from -0.0625 to 0.0625
- w_down: bfloat16 [8, 2048, 7168], P('group', 'inner'), may hold values from -0.125 to 0.125
Outputs:
- moe_out: bfloat16 [1024, 7168], P('group', 'inner')
Inputs may be any that keep to these rules, and one draw needn't show every extreme that they name: `routes`: each row names 4 different expert groups. Within each aligned block of 128 rows (the rows of one index of group) no group is named by more than 96 rows, and in some blocks one group is named by exactly 96 rows.
All inputs are finite; a program needn't handle non-finite values.
Results may differ from a plain program's by a relative error of at most 0.014.
Values may be sent and summed in bfloat16 or wider, within the bound.
No kernel may reach another device: no remote copies, remote signals or barrier semaphores. Data moves between devices by JAX's collectives and lax.ppermute only.
A program may use at most 128 MiB of HBM per device.

v0:
```python
import jax
import jax.numpy as jnp
from jax import lax
from jax.sharding import PartitionSpec as P


def layout(routes, groups, capacity):
    group_ids = jnp.arange(groups, dtype=jnp.int32)
    onehot = routes[:, :, None] == group_ids[None, None, :]
    chosen = jnp.sum(onehot.astype(jnp.int32), axis=1)
    slot_of = jnp.cumsum(chosen, axis=0) - 1
    slot_ids = jnp.arange(capacity, dtype=jnp.int32)
    placing = (chosen.T[:, None, :] == 1) & (slot_of.T[:, None, :] == slot_ids[None, :, None])
    pick_slot = jnp.take_along_axis(slot_of, routes, axis=1)
    pick_index = routes * capacity + pick_slot
    return (placing, pick_index)


def pack_rows(placing, token_rows):
    packed = jnp.einsum(
        "hct,td->hcd", placing.astype(jnp.bfloat16), token_rows, preferred_element_type=jnp.float32
    )
    return packed.astype(jnp.bfloat16)


def combine(pick_index, gate_weights, returned):
    flat_rows = returned.reshape(returned.shape[0] * returned.shape[1], returned.shape[2])
    taken = jnp.take(flat_rows, pick_index, axis=0)
    return jnp.sum(taken * gate_weights[:, :, None], axis=1)


def local(tokens, routes, gate_weights, w_gate, w_up, w_down):
    groups = lax.axis_size("group")
    shard_rows = tokens.shape[0]
    capacity = shard_rows * routes.shape[1] * 3 // (2 * groups)
    placing, pick_index = layout(routes, groups, capacity)
    gate_mat = w_gate[0]
    up_mat = w_up[0]
    down_mat = w_down[0]
    arrived = lax.all_to_all(
        pack_rows(placing, tokens), "group", split_axis=0, concat_axis=0, tiled=True
    )
    feature_part = lax.all_gather(arrived, "inner", axis=2, tiled=True)
    gate_add = jnp.einsum("hck,kf->hcf", feature_part, gate_mat, preferred_element_type=jnp.float32)
    up_add = jnp.einsum("hck,kf->hcf", feature_part, up_mat, preferred_element_type=jnp.float32)
    hidden = (jax.nn.silu(gate_add) * up_add).astype(jnp.bfloat16)
    partial_value = jnp.einsum(
        "hcf,fd->hcd", hidden, down_mat, preferred_element_type=jnp.float32
    ).astype(jnp.bfloat16)
    summed = lax.psum_scatter(partial_value, "inner", scatter_dimension=2, tiled=True).astype(
        jnp.float32
    )
    returned = lax.all_to_all(
        summed.astype(jnp.bfloat16), "group", split_axis=0, concat_axis=0, tiled=True
    ).astype(summed.dtype)
    result = combine(pick_index, gate_weights, returned).astype(jnp.bfloat16)
    return result


def solution(mesh):
    placed = (
        P("group", "inner"),
        P("group", None),
        P("group", None),
        P("group", None, "inner"),
        P("group", None, "inner"),
        P("group", "inner", None),
    )
    return jax.shard_map(
        local, mesh=mesh, in_specs=placed, out_specs=P("group", "inner"), check_vma=False
    )
```

profile of v0, /device:TPU:0, one launch (start us, length us, event | category | flops | bytes accessed | tf_op | source)
XLA Modules:
  0.0 366.3 jit_solution(16839487212041661017)
XLA Ops:
  6.5 0.7 convert_reduce_fusion
  7.3 0.1 copy.33
  7.4 0.2 reduce_window_sum.11
  7.6 0.9 convolution_convert_fusion.1
  8.5 69.8 %all_to_all.10 = bf16[8,96,1792]{2,1,0:T(8,128)(2,1)} all-to-all(bf16[8,96,1792]{2,1,0:T(8,128)(2,1)S(1)} %convolution_convert_fusion.1), channel_id=1, replica_groups=mesh['group'=8,'inner'=4] {'group'}, dimensions={0} | all-to-all | bytes 5505024 | tf_op jit(solution)/shard_map/all_to_all | solution.py:40
  78.4 71.9 %all-gather.2.cloned.1.call-done = bf16[8,96,7168]{2,1,0:T(8,128)(2,1)} async-done(((bf16[8,96,1792]{2,1,0:T(8,128)(2,1)}), bf16[8,96,7168]{2,1,0:T(8,128)(2,1)}) %all-gather.2.cloned.1.call-update) | async-done | bytes 11010064 | tf_op jit(solution)/shard_map/all_gather | solution.py:43
  150.4 10.9 %fusion.3 = f32[8,96,512]{2,1,0:T(8,128)S(1)} fusion(bf16[8,96,7168]{2,1,0:T(8,128)(2,1)} %all-gather.2.cloned.1.call-done, bf16[1,7168,512]{2,1,0:T(8,128)(2,1)} %param.9), kind=kOutput, calls=%fused_computation.6 | convolution fusion | flops 5637144576 | bytes 19922944 | tf_op jit(solution)/shard_map/hck,kf->hcf/dot_general | solution.py:44
  161.3 8.2 %multiply_convert_fusion = bf16[8,96,512]{2,1,0:T(8,128)(2,1)S(1)} fusion(f32[8,96,512]{2,1,0:T(8,128)S(1)} %fusion.3, bf16[8,96,7168]{2,1,0:T(8,128)(2,1)S(1)} %copy-done.4, bf16[1,7168,512]{2,1,0:T(8,128)(2,1)} %param.10), kind=kOutput, calls=%fused_computation.11 | convolution fusion | flops 5639503872 | bytes 20709376 | tf_op jit(solution)/shard_map/hck,kf->hcf/dot_general | solution.py:45
  169.5 11.6 %convolution_convert_fusion = bf16[8,96,7168]{2,1,0:T(8,128)(2,1)} fusion(bf16[8,96,512]{2,1,0:T(8,128)(2,1)S(1)} %multiply_convert_fusion, bf16[1,512,7168]{2,1,0:T(8,128)(2,1)} %param.11), kind=kOutput, calls=%fused_computation.2 | convolution fusion | flops 5642649600 | bytes 19136512 | tf_op jit(solution)/shard_map/hcf,fd->hcd/dot_general | solution.py:47
  181.1 88.9 %reduce-scatter.2.cloned.1.call-done = bf16[8,96,1792]{2,1,0:T(8,128)(2,1)} async-done(((bf16[8,96,7168]{2,1,0:T(8,128)(2,1)}), bf16[8,96,1792]{2,1,0:T(8,128)(2,1)}) %reduce-scatter.2.cloned.1.call-update) | async-done | bytes 2752528 | tf_op jit(solution)/shard_map/reduce_scatter | solution.py:50
  270.0 5.5 %all-to-all-start.1 = ((bf16[8,96,1792]{2,1,0:T(8,128)(2,1)}), bf16[8,96,1792]{2,1,0:T(8,128)(2,1)S(1)}, u32[]{:S(2)}, u32[]{:S(2)}) async-start(bf16[8,96,1792]{2,1,0:T(8,128)(2,1)} %reduce-scatter.2.cloned.1.call-done), calls=%async_computation.2 | async-start | bytes 5505024 | tf_op jit(solution)/shard_map/all_to_all | solution.py:53
  275.5 0.1 copy.34
  275.6 0.1 reshape.38
  275.7 3.8 %gather_fusion.1 = s32[512]{0:T(512)S(1)} fusion(s32[128,8]{1,0:T(8,128)S(1)} %get-tuple-element.7, s32[512]{0:T(512)S(1)} %reshape.38), kind=kCustom, calls=%fused_computation.1 | custom fusion | bytes 8192 | tf_op jit(solution)/shard_map/jit(take_along_axis)/gather | solution.py:14
  279.5 0.1 reshape.41
  279.7 0.1 copy.38
  279.8 0.1 reshape.32
  279.9 0.1 copy.36
  280.1 0.1 copy.39
  280.2 57.6 %all-to-all-done.1 = bf16[8,96,1792]{2,1,0:T(8,128)(2,1)S(1)} async-done(((bf16[8,96,1792]{2,1,0:T(8,128)(2,1)}), bf16[8,96,1792]{2,1,0:T(8,128)(2,1)S(1)}, u32[]{:S(2)}, u32[]{:S(2)}) %all-to-all-start.1) | async-done | bytes 2752544 | tf_op jit(solution)/shard_map/all_to_all | solution.py:53
  337.8 3.0 bitcast_convert_fusion
  340.7 7.5 %gather_fusion = f32[512,1792]{1,0:T(8,128)} fusion(f32[768,1792]{1,0:T(8,128)} %bitcast_convert_fusion, s32[1024]{0:T(1024)S(1)} %pad_clamp_fusion), kind=kCustom, calls=%fused_computation | custom fusion | bytes 7342080 | tf_op jit(solution)/shard_map/jit(_take)/gather | solution.py:28
  348.3 5.1 %reshape.31 = f32[128,4,1792]{2,1,0:T(4,128)} reshape(f32[512,1792]{1,0:T(8,128)} %gather_fusion) | data formatting | bytes 7340032 | tf_op jit(solution)/shard_map/jit(_take)/gather | solution.py:28
  353.4 6.0 %multiply_reduce_fusion = bf16[128,1792]{1,0:T(8,128)(2,1)} fusion(f32[128,4,1792]{2,1,0:T(4,128)} %reshape.31, f32[128,4]{1,0:T(8,128)S(1)} %copy.39, pred[128,4]{1,0:T(8,128)(4,1)S(1)} %copy.36), kind=kLoop, calls=%fused_computation.8 | loop fusion | flops 2523136 | bytes 4131328 | tf_op jit(solution)/shard_map/reduce_sum | solution.py:29
  (21 shorter events, 0.3 us)
Async XLA Ops:
  6.5 1.1 copy-start
  6.5 143.8 %all-gather.2.cloned.1.call-start = ((), (), s32[]{:S(2)}) async-start(), calls=%async_computation.3 | async-start | bytes 13762560 | tf_op jit(solution)/shard_map/all_gather | solution.py:43
  78.4 191.6 %reduce-scatter.2.cloned.1.call-start = ((), (), s32[]{:S(2)}) async-start(), calls=%async_computation.4 | async-start | bytes 13762560 | tf_op jit(solution)/shard_map/reduce_scatter | solution.py:50
  150.4 10.9 %copy-start.4 = (bf16[8,96,7168]{2,1,0:T(8,128)(2,1)S(1)}, bf16[8,96,7168]{2,1,0:T(8,128)(2,1)}, u32[]{:S(2)}) copy-start(bf16[8,96,7168]{2,1,0:T(8,128)(2,1)} %all-gather.2.cloned.1.call-done) | copy-start | bytes 33030148
  181.1 94.4 %copy-start.2 = (s32[128,4]{0,1:T(4,128)S(1)}, s32[128,4]{0,1:T(4,128)}, u32[]{:S(2)}) copy-start(s32[128,4]{0,1:T(4,128)} %param.7) | copy-start | bytes 6148
  270.0 67.8 %all-to-all-start.1 = ((bf16[8,96,1792]{2,1,0:T(8,128)(2,1)}), bf16[8,96,1792]{2,1,0:T(8,128)(2,1)S(1)}, u32[]{:S(2)}, u32[]{:S(2)}) async-start(bf16[8,96,1792]{2,1,0:T(8,128)(2,1)} %reduce-scatter.2.cloned.1.call-done), calls=%async_computation.2 | async-start | bytes 5505024 | tf_op jit(solution)/shard_map/all_to_all | solution.py:53
  275.7 4.4 %copy-start.3 = (f32[128,4]{0,1:T(4,128)S(1)}, f32[128,4]{0,1:T(4,128)}, u32[]{:S(2)}) copy-start(f32[128,4]{0,1:T(4,128)} %param.8) | copy-start | bytes 6148
  348.3 11.2 %copy-start.1 = (bf16[128,1792]{1,0:T(8,128)(2,1)S(1)}, bf16[128,1792]{1,0:T(8,128)(2,1)}, u32[]{:S(2)}) copy-start(bf16[128,1792]{1,0:T(8,128)(2,1)} %param.6) | copy-start | bytes 1376260
Sparse Core Ops, SparseCore 0:
  78.5 71.7 all-gather.1
  181.2 88.7 reduce-scatter.1
where the time goes:
time: 367 us; the launch traced here: 366 us
  waiting for transfers between devices  218 us (59%)
  blocking collectives  69.8 us (19%)
  matrix products  31.5 us (9%)
  local copies, waits for them, and re-layouts  17.5 us (5%)
  between operations  13.5 us (4%)
  other arithmetic  9.95 us (3%)
  starting transfers between devices  5.56 us (2%)
    reduce_scatter x1, waiting for transfers between devices, local(): lax.psum_scatter(partial_value, 'inner', scatter_dimension=2, tiled=True)  88.9 us
    all_gather x1, waiting for transfers between devices, local(): feature_part = lax.all_gather(arrived, 'inner', axis=2, tiled=True)  71.9 us
    all_to_all x1, blocking collectives, local(): lax.all_to_all(pack_rows(placing, tokens), 'group', split_axis=0, concat_...  69.8 us
    all_to_all x1, waiting for transfers between devices, local(): lax.all_to_all(summed.astype(jnp.bfloat16), 'group', split_axis=0, concat...  57.6 us
    gather x2, local copies, waits for them, and re-layouts, combine(): taken = jnp.take(flat_rows, pick_index, axis=0)  12.7 us
    dot_general x1, matrix products, local(): jnp.einsum('hcf,fd->hcd', hidden, down_mat, preferred_element_type=jnp.fl...  11.6 us
    dot_general x1, matrix products, local(): jnp.einsum('hck,kf->hcf', feature_part, gate_mat, preferred_element_type=...  10.9 us
    dot_general x1, matrix products, local(): jnp.einsum('hck,kf->hcf', feature_part, up_mat, preferred_element_type=jn...  8.21 us
  transfers between devices with their start and end apart: 3, of which 3 were waited for; matrix products, arithmetic and copies ran while one was open for 1% of the time, Pallas kernels for 0%

commit v1 on v0

v1 whole, which is shorter than its diff:
```python
import jax
import jax.numpy as jnp
from jax import lax
from jax.sharding import PartitionSpec as P

BF = jnp.bfloat16
F32 = jnp.float32


def routing(routes, gate_weights, groups):
    onehot = routes[:, :, None] == jnp.arange(groups, dtype=jnp.int32)
    weight = jnp.sum(jnp.where(onehot, gate_weights[:, :, None], 0.0), axis=1).T
    picked = jnp.any(onehot, axis=1).T
    rows = routes.shape[0]
    before = jnp.arange(rows)[:, None] < jnp.arange(rows)[None, :]
    slot = jnp.dot(picked.astype(BF), before.astype(BF), preferred_element_type=F32)
    return jnp.stack([jnp.where(picked, slot, -1.0), weight])


def local(tokens, routes, gate_weights, w_gate, w_up, w_down):
    groups, inners = lax.axis_size("group"), lax.axis_size("inner")
    g, i = lax.axis_index("group"), lax.axis_index("inner")
    chips, planes = inners // 2, groups // 2
    x, c = i // 2, i % 2
    rows, feats = tokens.shape
    cap = rows * routes.shape[1] * 3 // (2 * groups)
    depth = w_down.shape[2]

    def over_y(a):
        return lax.ppermute(a, "group", [(j, j ^ 1) for j in range(groups)])

    def over_z(a):
        return lax.ppermute(a, "group", [(j, (j + 2) % groups) for j in range(groups)])

    def over_core(a):
        return lax.ppermute(a, "inner", [(j, j ^ 1) for j in range(inners)])

    def over_x(a, s):
        return lax.ppermute(a, "inner", [(j, (j + 2 * s) % inners) for j in range(inners)])

    info = routing(routes, gate_weights, groups)
    infos = [jnp.stack([info, over_y(info)])]
    main = [tokens]
    for t in range(1, planes):
        infos.append(over_z(infos[-1]))
        main.append(over_z(main[-1]))
    other = [over_y(a) for a in main]

    slots = jnp.arange(cap, dtype=jnp.int32).astype(F32)
    q = []
    for t in range(planes):
        mine = lax.dynamic_index_in_dim(infos[t], g, 2, keepdims=False)
        packed, parts = [], [[] for _ in range(chips)]
        for u, block in enumerate((main[t], other[t])):
            placing = (mine[u, 0][None, :] == slots[:, None]).astype(BF)
            p = jnp.dot(placing, block, preferred_element_type=F32).astype(BF)
            for s in range(chips):
                parts[s].append(p if s == 0 else over_x(p, s))
        parts = [jnp.concatenate(p, axis=0) for p in parts]
        ordered = []
        for k in range(chips):
            value = parts[0]
            for s in range(1, chips):
                value = jnp.where((x - s) % chips == k, parts[s], value)
            ordered.append(value)
        half = jnp.stack(ordered, axis=1)
        far = over_core(half)
        even, odd = jnp.where(c == 0, half, far), jnp.where(c == 0, far, half)
        full = jnp.stack([even, odd], axis=2).reshape(2 * cap, depth)
        gate = jnp.dot(full, w_gate[0], preferred_element_type=F32)
        up = jnp.dot(full, w_up[0], preferred_element_type=F32)
        hidden = (jax.nn.silu(gate) * up).astype(BF)
        part = jnp.dot(hidden, w_down[0], preferred_element_type=F32).astype(BF)
        part = part.reshape(2 * cap, chips, 2, feats)
        keep = jnp.where(c == 0, part[:, :, 0], part[:, :, 1])
        give = jnp.where(c == 0, part[:, :, 1], part[:, :, 0])
        pair = keep.astype(F32) + over_core(give).astype(F32)
        weighted = []
        for u in (0, 1):
            here = pair[u * cap:(u + 1) * cap]
            total = lax.dynamic_index_in_dim(here, x, 1, keepdims=False)
            for s in range(1, chips):
                away = lax.dynamic_index_in_dim(here, (x + s) % chips, 1, keepdims=False)
                total = total + over_x(away.astype(BF), s).astype(F32)
            back = (mine[u, 0][:, None] == slots[None, :]).astype(BF)
            spread = jnp.dot(back, total.astype(BF), preferred_element_type=F32)
            weighted.append(spread * mine[u, 1][:, None])
        q.append(weighted[0] + over_y(weighted[1].astype(BF)).astype(F32))

    total = q[1 % planes]
    for t in range(2, planes + 1):
        total = over_z(total.astype(BF)).astype(F32) + q[t % planes]
    return total.astype(BF)


def solution(mesh):
    placed = (
        P("group", "inner"),
        P("group", None),
        P("group", None),
        P("group", None, "inner"),
        P("group", None, "inner"),
        P("group", "inner", None),
    )
    return jax.shard_map(
        local, mesh=mesh, in_specs=placed, out_specs=P("group", "inner"), check_vma=False
    )
```

time: 367 us -> 368 us (level)
  waiting for transfers between devices: 218 us -> 104 us
  local copies, waits for them, and re-layouts: 17.5 us -> 124 us
  blocking collectives: 69.8 us -> 0 us
  matrix products: 31.5 us -> 70.8 us
  starting transfers between devices: 5.56 us -> 42.5 us
  other arithmetic: 9.95 us -> 23.1 us
  between operations: 13.5 us -> 0.88 us
    ppermute x0 -> x42, waiting for transfers between devices: none -> 104 us  [the longest x16 61.6 us: over_x(): lax.ppermute(a, 'inner', [(j, (j + 2 * s) % inners) for j in range(inners)])]
    reduce_scatter x1 -> x0, waiting for transfers between devices: 88.9 us -> none  [local(): lax.psum_scatter(partial_value, 'inner', scatter_dimension=2, tiled=True)]
    all_gather x1 -> x0, waiting for transfers between devices: 71.9 us -> none  [local(): feature_part = lax.all_gather(arrived, 'inner', axis=2, tiled=True)]
    all_to_all x1 -> x0, blocking collectives: 69.8 us -> none  [local(): lax.all_to_all(pack_rows(placing, tokens), 'group', split_axis=0, concat_...]
    reshape x0 -> x8, local copies, waits for them, and re-layouts: none -> 69.3 us  [the longest x4 39.5 us: local(): full = jnp.stack([even, odd], axis=2).reshape(2 * cap, depth)]
    all_to_all x1 -> x0, waiting for transfers between devices: 57.6 us -> none  [local(): lax.all_to_all(summed.astype(jnp.bfloat16), 'group', split_axis=0, concat...]
    ppermute x0 -> x42, starting transfers between devices: none -> 42.5 us  [the longest x16 23.3 us: over_x(): lax.ppermute(a, 'inner', [(j, (j + 2 * s) % inners) for j in range(inners)])]
    dot_general x4 -> x25, matrix products: 31.5 us -> 70.8 us  [the longest x4 41.9 us: local(): part = jnp.dot(hidden, w_down[0], preferred_element_type=F32).astype(BF)]
  transfers between devices with their start and end apart: 3 -> 42, of which waited for: 3 -> 20; matrix products, arithmetic and copies ran while one was open for 1% -> 58% of each run, Pallas kernels for 0% -> 0%
where the time goes in v1:
time: 368 us; the launch traced here: 366 us
  local copies, waits for them, and re-layouts  124 us (34%)
  waiting for transfers between devices  104 us (28%)
  matrix products  70.8 us (19%)
  starting transfers between devices  42.5 us (12%)
  other arithmetic  23.1 us (6%)
    ppermute x16, waiting for transfers between devices, over_x(): lax.ppermute(a, 'inner', [(j, (j + 2 * s) % inners) for j in range(inners)])  61.6 us
    dot_general x4, matrix products, local(): part = jnp.dot(hidden, w_down[0], preferred_element_type=F32).astype(BF)  41.9 us
    reshape x4, local copies, waits for them, and re-layouts, local(): full = jnp.stack([even, odd], axis=2).reshape(2 * cap, depth)  39.5 us
    reshape x4, local copies, waits for them, and re-layouts, local(): part = part.reshape(2 * cap, chips, 2, feats)  29.8 us
    slice x4, local copies, waits for them, and re-layouts, local(): keep = jnp.where(c == 0, part[:, :, 0], part[:, :, 1])  29.8 us
    ppermute x9, waiting for transfers between devices, over_y(): return lax.ppermute(a, 'group', [(j, j ^ 1) for j in range(groups)])  23.4 us
    ppermute x16, starting transfers between devices, over_x(): lax.ppermute(a, 'inner', [(j, (j + 2 * s) % inners) for j in range(inners)])  23.3 us
    dot_general x4, matrix products, local(): gate = jnp.dot(full, w_gate[0], preferred_element_type=F32)  21.9 us
  transfers between devices with their start and end apart: 42, of which 20 were waited for; matrix products, arithmetic and copies ran while one was open for 58% of the time, Pallas kernels for 0%

profile of v1, /device:TPU:0, one launch (start us, length us, event | category | flops | bytes accessed | tf_op | source)
XLA Modules:
  0.0 365.5 jit_solution(13066022336199349018)
XLA Ops:
  6.6 8.8 %collective-permute-done = f32[2,8,128]{2,1,0:T(8,128)S(1)} collective-permute-done((f32[2,8,128]{2,1,0:T(8,128)S(1)}, f32[2,8,128]{2,1,0:T(8,128)S(1)}, u32[]{:S(2)}, u32[]{:S(2)}) %collective-permute-start) | collective-permute-done | bytes 8224 | tf_op jit(solution)/shard_map/ppermute | solution.py:30
  26.5 5.5 %collective-permute-done.23 = f32[2,2,8,128]{3,2,1,0:T(8,128)S(1)} collective-permute-done((f32[2,2,8,128]{3,2,1,0:T(8,128)S(1)}, f32[2,2,8,128]{3,2,1,0:T(8,128)S(1)}, u32[]{:S(2)}, u32[]{:S(2)}) %collective-permute-start.23) | collective-permute-done | bytes 16416 | tf_op jit(solution)/shard_map/ppermute | solution.py:33
  36.3 6.7 %collective-permute-done.36 = bf16[96,1792]{1,0:T(8,128)(2,1)S(1)} collective-permute-done((bf16[96,1792]{1,0:T(8,128)(2,1)S(1)}, bf16[96,1792]{1,0:T(8,128)(2,1)S(1)}, u32[]{:S(2)}, u32[]{:S(2)}) %collective-permute-start.36) | collective-permute-done | bytes 344096 | tf_op jit(solution)/shard_map/ppermute | solution.py:39
  64.7 6.6 %collective-permute-done.26 = bf16[128,1792]{1,0:T(8,128)(2,1)S(1)} collective-permute-done((bf16[128,1792]{1,0:T(8,128)(2,1)S(1)}, bf16[128,1792]{1,0:T(8,128)(2,1)S(1)}, u32[]{:S(2)}, u32[]{:S(2)}) %collective-permute-start.26) | collective-permute-done | bytes 458784 | tf_op jit(solution)/shard_map/ppermute | solution.py:30
  76.1 7.0 %collective-permute-done.25 = bf16[96,1792]{1,0:T(8,128)(2,1)S(1)} collective-permute-done((bf16[96,1792]{1,0:T(8,128)(2,1)S(1)}, bf16[96,1792]{1,0:T(8,128)(2,1)S(1)}, u32[]{:S(2)}, u32[]{:S(2)}) %collective-permute-start.25) | collective-permute-done | bytes 344096 | tf_op jit(solution)/shard_map/ppermute | solution.py:39
  95.1 6.1 %reshape.536 = bf16[192,7168]{1,0:T(8,128)(2,1)S(1)} reshape(bf16[192,2,2,1792]{3,2,1,0:T(2,128)(2,1)} %copy.42) | data formatting | bytes 5505024 | tf_op jit(solution)/shard_map/reshape | solution.py:69
  106.7 10.0 %convolution_convert_fusion = bf16[192,7168]{1,0:T(8,128)(2,1)} fusion(bf16[1,512,7168]{2,1,0:T(8,128)(2,1)} %param.11, bf16[192,7168]{1,0:T(8,128)(2,1)S(1)} %reshape.536, bf16[1,7168,512]{2,1,0:T(8,128)(2,1)} %param.10, f32[192,512]{1,0:T(8,128)} %fusion.12), kind=kOutput, calls=%fused_computation | convolution fusion | flops 2820538368 | bytes 20578304 | tf_op jit(solution)/shard_map/dot_general | solution.py:73
  116.6 7.7 %reshape.537 = bf16[192,2,2,1792]{3,2,1,0:T(2,128)(2,1)} reshape(bf16[192,7168]{1,0:T(8,128)(2,1)} %convolution_convert_fusion) | data formatting | bytes 5505024 | tf_op jit(solution)/shard_map/reshape | solution.py:74
  124.3 7.4 %fusion.178 = (bf16[192,2,1,1792]{3,2,1,0:T(2,128)(2,1)S(1)}, bf16[192,2,1,1792]{3,2,1,0:T(2,128)(2,1)S(1)}) fusion(bf16[192,2,2,1792]{3,2,1,0:T(2,128)(2,1)} %reshape.537), kind=kLoop, calls=%fused_computation.247 | loop fusion | bytes 5505024 | tf_op jit(solution)/shard_map/slice | solution.py:75
  140.4 18.6 %reshape.530 = bf16[192,7168]{1,0:T(8,128)(2,1)} reshape(bf16[192,2,2,1792]{3,2,1,0:T(2,128)(2,1)} %copy.33) | data formatting | bytes 5505024 | tf_op jit(solution)/shard_map/reshape | solution.py:69
  164.5 10.7 %convolution_convert_fusion.3 = bf16[192,7168]{1,0:T(8,128)(2,1)} fusion(bf16[1,512,7168]{2,1,0:T(8,128)(2,1)} %param.11, bf16[192,7168]{1,0:T(8,128)(2,1)} %reshape.530, bf16[1,7168,512]{2,1,0:T(8,128)(2,1)} %param.10, f32[192,512]{1,0:T(8,128)S(1)} %fusion.18), kind=kOutput, calls=%fused_computation.3 | convolution fusion | flops 2820538368 | bytes 20578304 | tf_op jit(solution)/shard_map/dot_general | solution.py:73
  175.1 7.4 %reshape.531 = bf16[192,2,2,1792]{3,2,1,0:T(2,128)(2,1)} reshape(bf16[192,7168]{1,0:T(8,128)(2,1)} %convolution_convert_fusion.3) | data formatting | bytes 5505024 | tf_op jit(solution)/shard_map/reshape | solution.py:74
  182.5 7.4 %fusion.180 = (bf16[192,2,1,1792]{3,2,1,0:T(2,128)(2,1)S(1)}, bf16[192,2,1,1792]{3,2,1,0:T(2,128)(2,1)S(1)}) fusion(bf16[192,2,2,1792]{3,2,1,0:T(2,128)(2,1)} %reshape.531), kind=kLoop, calls=%fused_computation.249 | loop fusion | bytes 5505024 | tf_op jit(solution)/shard_map/slice | solution.py:75
  199.1 7.5 %reshape.532 = bf16[192,7168]{1,0:T(8,128)(2,1)} reshape(bf16[192,2,2,1792]{3,2,1,0:T(2,128)(2,1)} %copy.36) | data formatting | bytes 5505024 | tf_op jit(solution)/shard_map/reshape | solution.py:69
  212.1 10.7 %convolution_convert_fusion.2 = bf16[192,7168]{1,0:T(8,128)(2,1)} fusion(bf16[1,512,7168]{2,1,0:T(8,128)(2,1)} %param.11, bf16[192,7168]{1,0:T(8,128)(2,1)} %reshape.532, bf16[1,7168,512]{2,1,0:T(8,128)(2,1)} %param.10, f32[192,512]{1,0:T(8,128)S(1)} %fusion.16), kind=kOutput, calls=%fused_computation.2 | convolution fusion | flops 2820538368 | bytes 20578304 | tf_op jit(solution)/shard_map/dot_general | solution.py:73
  222.8 7.4 %reshape.533 = bf16[192,2,2,1792]{3,2,1,0:T(2,128)(2,1)} reshape(bf16[192,7168]{1,0:T(8,128)(2,1)} %convolution_convert_fusion.2) | data formatting | bytes 5505024 | tf_op jit(solution)/shard_map/reshape | solution.py:74
  230.2 7.4 %fusion.182 = (bf16[192,2,1,1792]{3,2,1,0:T(2,128)(2,1)S(1)}, bf16[192,2,1,1792]{3,2,1,0:T(2,128)(2,1)S(1)}) fusion(bf16[192,2,2,1792]{3,2,1,0:T(2,128)(2,1)} %reshape.533), kind=kLoop, calls=%fused_computation.251 | loop fusion | bytes 5505024 | tf_op jit(solution)/shard_map/slice | solution.py:75
  247.1 7.3 %reshape.534 = bf16[192,7168]{1,0:T(8,128)(2,1)} reshape(bf16[192,2,2,1792]{3,2,1,0:T(2,128)(2,1)} %copy.39) | data formatting | bytes 5505024 | tf_op jit(solution)/shard_map/reshape | solution.py:69
  259.9 10.6 %convolution_convert_fusion.1 = bf16[192,7168]{1,0:T(8,128)(2,1)} fusion(bf16[1,512,7168]{2,1,0:T(8,128)(2,1)} %param.11, bf16[192,7168]{1,0:T(8,128)(2,1)} %reshape.534, bf16[1,7168,512]{2,1,0:T(8,128)(2,1)} %param.10, f32[192,512]{1,0:T(8,128)S(1)} %fusion.14), kind=kOutput, calls=%fused_computation.1 | convolution fusion | flops 2820538368 | bytes 20578304 | tf_op jit(solution)/shard_map/dot_general | solution.py:73
  270.5 7.4 %reshape.535 = bf16[192,2,2,1792]{3,2,1,0:T(2,128)(2,1)} reshape(bf16[192,7168]{1,0:T(8,128)(2,1)} %convolution_convert_fusion.1) | data formatting | bytes 5505024 | tf_op jit(solution)/shard_map/reshape | solution.py:74
  277.9 7.4 %fusion.184 = (bf16[192,2,1,1792]{3,2,1,0:T(2,128)(2,1)S(1)}, bf16[192,2,1,1792]{3,2,1,0:T(2,128)(2,1)S(1)}) fusion(bf16[192,2,2,1792]{3,2,1,0:T(2,128)(2,1)} %reshape.535), kind=kLoop, calls=%fused_computation.253 | loop fusion | bytes 5505024 | tf_op jit(solution)/shard_map/slice | solution.py:75
  299.8 7.8 %collective-permute-done.9 = bf16[96,1792]{1,0:T(8,128)(2,1)S(1)} collective-permute-done((bf16[96,1792]{1,0:T(8,128)(2,1)S(1)}, bf16[96,1792]{1,0:T(8,128)(2,1)S(1)}, u32[]{:S(2)}, u32[]{:S(2)}) %collective-permute-start.9) | collective-permute-done | bytes 344096 | tf_op jit(solution)/shard_map/ppermute | solution.py:39
  310.0 11.4 %collective-permute-done.20 = bf16[96,1792]{1,0:T(8,128)(2,1)S(1)} collective-permute-done((bf16[96,1792]{1,0:T(8,128)(2,1)S(1)}, bf16[96,1792]{1,0:T(8,128)(2,1)S(1)}, u32[]{:S(2)}, u32[]{:S(2)}) %collective-permute-start.20) | collective-permute-done | bytes 344096 | tf_op jit(solution)/shard_map/ppermute | solution.py:39
  345.6 8.0 %collective-permute-done.32 = bf16[128,1792]{1,0:T(8,128)(2,1)S(1)} collective-permute-done((bf16[128,1792]{1,0:T(8,128)(2,1)S(1)}, bf16[128,1792]{1,0:T(8,128)(2,1)S(1)}, u32[]{:S(2)}, u32[]{:S(2)}) %collective-permute-start.32) | collective-permute-done | bytes 458784 | tf_op jit(solution)/shard_map/ppermute | solution.py:30
  (192 shorter events, 161.8 us)
Async XLA Ops:
  0.0 33.9 %collective-permute-start.2 = (bf16[128,1792]{1,0:T(8,128)(2,1)}, bf16[128,1792]{1,0:T(8,128)(2,1)S(1)}, u32[]{:S(2)}, u32[]{:S(2)}) collective-permute-start(bf16[128,1792]{1,0:T(8,128)(2,1)} %param.6), channel_id=1, source_target_pairs={{0,8},{4,12},{8,16},{12,20},{16,24},{20,28},{24,0},{28,4},{1,9},{5... | collective-permute-start | bytes 1376264 | tf_op jit(solution)/shard_map/ppermute | solution.py:33
  3.0 29.0 %collective-permute-start.35 = (bf16[128,1792]{1,0:T(8,128)(2,1)}, bf16[128,1792]{1,0:T(8,128)(2,1)S(1)}, u32[]{:S(2)}, u32[]{:S(2)}) collective-permute-start(bf16[128,1792]{1,0:T(8,128)(2,1)} %param.6), channel_id=1, source_target_pairs={{0,4},{4,0},{8,12},{12,8},{16,20},{20,16},{24,28},{28,24},{1,5},{5... | collective-permute-start | bytes 1376264 | tf_op jit(solution)/shard_map/ppermute | solution.py:30
  18.3 18.0 %collective-permute-start.34 = (bf16[96,1792]{1,0:T(8,128)(2,1)S(1)}, bf16[96,1792]{1,0:T(8,128)(2,1)S(1)}, u32[]{:S(2)}, u32[]{:S(2)}) collective-permute-start(bf16[96,1792]{1,0:T(8,128)(2,1)S(1)} %convolution_convert_fusion.5), channel_id=1, source_target_pairs={{0,2},{1,3},{2,0},{3,1},{4,6},{5,7},{6,4},{7,5},{8,10},{9,11},{10,... | collective-permute-start | bytes 1032200 | tf_op jit(solution)/shard_map/ppermute | solution.py:39
  45.6 44.7 %collective-permute-start.37 = (bf16[192,2,1792]{2,0,1:T(8,128)(2,1)S(1)}, bf16[192,2,1792]{2,0,1:T(8,128)(2,1)S(1)}, u32[]{:S(2)}, u32[]{:S(2)}) collective-permute-start(bf16[192,2,1792]{2,0,1:T(8,128)(2,1)S(1)} %pad_maximum_fusion.7), channel_id=1, source_target_pairs={{0,1},{1,0},{2,3},{3,2},{4,5},{5,4},{6,7},{7,6},{8,9},{9,8},{10,11... | collective-permute-start | bytes 4128776 | tf_op jit(solution)/shard_map/ppermute | solution.py:36
  46.9 27.5 %collective-permute-start.14 = (bf16[96,1792]{1,0:T(8,128)(2,1)S(1)}, bf16[96,1792]{1,0:T(8,128)(2,1)S(1)}, u32[]{:S(2)}, u32[]{:S(2)}) collective-permute-start(bf16[96,1792]{1,0:T(8,128)(2,1)S(1)} %convolution_convert_fusion.9), channel_id=1, source_target_pairs={{0,2},{1,3},{2,0},{3,1},{4,6},{5,7},{6,4},{7,5},{8,10},{9,11},{10,... | collective-permute-start | bytes 1032200 | tf_op jit(solution)/shard_map/ppermute | solution.py:39
  48.6 13.8 %collective-permute-start.15 = (bf16[128,1792]{1,0:T(8,128)(2,1)S(1)}, bf16[128,1792]{1,0:T(8,128)(2,1)S(1)}, u32[]{:S(2)}, u32[]{:S(2)}) collective-permute-start(bf16[128,1792]{1,0:T(8,128)(2,1)S(1)} %collective-permute-done.13), channel_id=1, source_target_pairs={{0,4},{4,0},{8,12},{12,8},{16,20},{20,16},{24,28},{28,24},{1,5},{5... | collective-permute-start | bytes 1376264 | tf_op jit(solution)/shard_map/ppermute | solution.py:30
  57.0 77.2 %collective-permute-start.6 = (bf16[192,2,1792]{2,0,1:T(8,128)(2,1)}, bf16[192,2,1792]{2,0,1:T(8,128)(2,1)}, u32[]{:S(2)}, u32[]{:S(2)}) collective-permute-start(bf16[192,2,1792]{2,0,1:T(8,128)(2,1)} %pad_maximum_fusion.4), channel_id=1, source_target_pairs={{0,1},{1,0},{2,3},{3,2},{4,5},{5,4},{6,7},{7,6},{8,9},{9,8},{10,11... | collective-permute-start | bytes 4128776 | tf_op jit(solution)/shard_map/ppermute | solution.py:36
  74.4 13.5 %collective-permute-start.27 = (bf16[96,1792]{1,0:T(8,128)(2,1)S(1)}, bf16[96,1792]{1,0:T(8,128)(2,1)S(1)}, u32[]{:S(2)}, u32[]{:S(2)}) collective-permute-start(bf16[96,1792]{1,0:T(8,128)(2,1)S(1)} %convolution_convert_fusion.6), channel_id=1, source_target_pairs={{0,2},{1,3},{2,0},{3,1},{4,6},{5,7},{6,4},{7,5},{8,10},{9,11},{10,... | collective-permute-start | bytes 1032200 | tf_op jit(solution)/shard_map/ppermute | solution.py:39
  76.1 116.7 %collective-permute-start.17 = (bf16[192,2,1792]{2,0,1:T(8,128)(2,1)}, bf16[192,2,1792]{2,0,1:T(8,128)(2,1)}, u32[]{:S(2)}, u32[]{:S(2)}) collective-permute-start(bf16[192,2,1792]{2,0,1:T(8,128)(2,1)} %pad_maximum_fusion.5), channel_id=1, source_target_pairs={{0,1},{1,0},{2,3},{3,2},{4,5},{5,4},{6,7},{7,6},{8,9},{9,8},{10,11... | collective-permute-start | bytes 4128776 | tf_op jit(solution)/shard_map/ppermute | solution.py:36
  90.3 150.6 %collective-permute-start.28 = (bf16[192,2,1792]{2,0,1:T(8,128)(2,1)}, bf16[192,2,1792]{2,0,1:T(8,128)(2,1)}, u32[]{:S(2)}, u32[]{:S(2)}) collective-permute-start(bf16[192,2,1792]{2,0,1:T(8,128)(2,1)} %pad_maximum_fusion.6), channel_id=1, source_target_pairs={{0,1},{1,0},{2,3},{3,2},{4,5},{5,4},{6,7},{7,6},{8,9},{9,8},{10,11... | collective-permute-start | bytes 4128776 | tf_op jit(solution)/shard_map/ppermute | solution.py:36
  133.7 152.1 %collective-permute-start.38 = (bf16[192,2,1792]{2,0,1:T(8,128)(2,1)}, bf16[192,2,1792]{2,0,1:T(8,128)(2,1)}, u32[]{:S(2)}, u32[]{:S(2)}) collective-permute-start(bf16[192,2,1792]{2,0,1:T(8,128)(2,1)} %select_bitcast_fusion), channel_id=1, source_target_pairs={{0,1},{1,0},{2,3},{3,2},{4,5},{5,4},{6,7},{7,6},{8,9},{9,8},{10,11... | collective-permute-start | bytes 4128776 | tf_op jit(solution)/shard_map/ppermute | solution.py:36
  192.8 98.2 %collective-permute-start.7 = (bf16[192,2,1792]{2,0,1:T(8,128)(2,1)}, bf16[192,2,1792]{2,0,1:T(8,128)(2,1)}, u32[]{:S(2)}, u32[]{:S(2)}) collective-permute-start(bf16[192,2,1792]{2,0,1:T(8,128)(2,1)} %select_bitcast_fusion.9), channel_id=1, source_target_pairs={{0,1},{1,0},{2,3},{3,2},{4,5},{5,4},{6,7},{7,6},{8,9},{9,8},{10,11... | collective-permute-start | bytes 4128776 | tf_op jit(solution)/shard_map/ppermute | solution.py:36
  240.4 55.4 %collective-permute-start.18 = (bf16[192,2,1792]{2,0,1:T(8,128)(2,1)}, bf16[192,2,1792]{2,0,1:T(8,128)(2,1)}, u32[]{:S(2)}, u32[]{:S(2)}) collective-permute-start(bf16[192,2,1792]{2,0,1:T(8,128)(2,1)} %select_bitcast_fusion.6), channel_id=1, source_target_pairs={{0,1},{1,0},{2,3},{3,2},{4,5},{5,4},{6,7},{7,6},{8,9},{9,8},{10,11... | collective-permute-start | bytes 4128776 | tf_op jit(solution)/shard_map/ppermute | solution.py:36
  285.7 40.2 %collective-permute-start.29 = (bf16[192,2,1792]{2,0,1:T(8,128)(2,1)S(1)}, bf16[192,2,1792]{2,0,1:T(8,128)(2,1)S(1)}, u32[]{:S(2)}, u32[]{:S(2)}) collective-permute-start(bf16[192,2,1792]{2,0,1:T(8,128)(2,1)S(1)} %select_bitcast_fusion.3), channel_id=1, source_target_pairs={{0,1},{1,0},{2,3},{3,2},{4,5},{5,4},{6,7},{7,6},{8,9},{9,8},{10,11... | collective-permute-start | bytes 4128776 | tf_op jit(solution)/shard_map/ppermute | solution.py:36
  289.2 53.2 %collective-permute-start.40 = (bf16[96,1792]{1,0:T(8,128)(2,1)S(1)}, bf16[96,1792]{1,0:T(8,128)(2,1)S(1)}, u32[]{:S(2)}, u32[]{:S(2)}) collective-permute-start(bf16[96,1792]{1,0:T(8,128)(2,1)S(1)} %fusion.93), channel_id=1, source_target_pairs={{0,2},{1,3},{2,0},{3,1},{4,6},{5,7},{6,4},{7,5},{8,10},{9,11},{10,... | collective-permute-start | bytes 1032200 | tf_op jit(solution)/shard_map/ppermute | solution.py:39
  293.6 14.0 %collective-permute-start.9 = (bf16[96,1792]{1,0:T(8,128)(2,1)S(1)}, bf16[96,1792]{1,0:T(8,128)(2,1)S(1)}, u32[]{:S(2)}, u32[]{:S(2)}) collective-permute-start(bf16[96,1792]{1,0:T(8,128)(2,1)S(1)} %fusion.87), channel_id=1, source_target_pairs={{0,2},{1,3},{2,0},{3,1},{4,6},{5,7},{6,4},{7,5},{8,10},{9,11},{10,... | collective-permute-start | bytes 1032200 | tf_op jit(solution)/shard_map/ppermute | solution.py:39
  295.5 28.0 %collective-permute-start.8 = (bf16[96,1792]{1,0:T(8,128)(2,1)S(1)}, bf16[96,1792]{1,0:T(8,128)(2,1)S(1)}, u32[]{:S(2)}, u32[]{:S(2)}) collective-permute-start(bf16[96,1792]{1,0:T(8,128)(2,1)S(1)} %fusion.86), channel_id=1, source_target_pairs={{0,2},{1,3},{2,0},{3,1},{4,6},{5,7},{6,4},{7,5},{8,10},{9,11},{10,... | collective-permute-start | bytes 1032200 | tf_op jit(solution)/shard_map/ppermute | solution.py:39
  298.0 23.4 %collective-permute-start.20 = (bf16[96,1792]{1,0:T(8,128)(2,1)S(1)}, bf16[96,1792]{1,0:T(8,128)(2,1)S(1)}, u32[]{:S(2)}, u32[]{:S(2)}) collective-permute-start(bf16[96,1792]{1,0:T(8,128)(2,1)S(1)} %fusion.89), channel_id=1, source_target_pairs={{0,2},{1,3},{2,0},{3,1},{4,6},{5,7},{6,4},{7,5},{8,10},{9,11},{10,... | collective-permute-start | bytes 1032200 | tf_op jit(solution)/shard_map/ppermute | solution.py:39
  307.9 17.6 %collective-permute-start.10 = (bf16[128,1792]{1,0:T(8,128)(2,1)S(1)}, bf16[128,1792]{1,0:T(8,128)(2,1)S(1)}, u32[]{:S(2)}, u32[]{:S(2)}) collective-permute-start(bf16[128,1792]{1,0:T(8,128)(2,1)S(1)} %fusion.23), channel_id=1, source_target_pairs={{0,4},{4,0},{8,12},{12,8},{16,20},{20,16},{24,28},{28,24},{1,5},{5... | collective-permute-start | bytes 1376264 | tf_op jit(solution)/shard_map/ppermute | solution.py:30
  323.5 18.7 %collective-permute-start.21 = (bf16[128,1792]{1,0:T(8,128)(2,1)S(1)}, bf16[128,1792]{1,0:T(8,128)(2,1)S(1)}, u32[]{:S(2)}, u32[]{:S(2)}) collective-permute-start(bf16[128,1792]{1,0:T(8,128)(2,1)S(1)} %multiply_convert_fusion.1), channel_id=1, source_target_pairs={{0,4},{4,0},{8,12},{12,8},{16,20},{20,16},{24,28},{28,24},{1,5},{5... | collective-permute-start | bytes 1376264 | tf_op jit(solution)/shard_map/ppermute | solution.py:30
  325.8 16.3 %collective-permute-start.11 = (bf16[128,1792]{1,0:T(8,128)(2,1)S(1)}, bf16[128,1792]{1,0:T(8,128)(2,1)S(1)}, u32[]{:S(2)}, u32[]{:S(2)}) collective-permute-start(bf16[128,1792]{1,0:T(8,128)(2,1)S(1)} %fusion.22), channel_id=1, source_target_pairs={{0,8},{4,12},{8,16},{12,20},{16,24},{20,28},{24,0},{28,4},{1,9},{5... | collective-permute-start | bytes 1376264 | tf_op jit(solution)/shard_map/ppermute | solution.py:33
  326.7 13.1 %collective-permute-start.31 = (bf16[96,1792]{1,0:T(8,128)(2,1)S(1)}, bf16[96,1792]{1,0:T(8,128)(2,1)S(1)}, u32[]{:S(2)}, u32[]{:S(2)}) collective-permute-start(bf16[96,1792]{1,0:T(8,128)(2,1)S(1)} %fusion.91), channel_id=1, source_target_pairs={{0,2},{1,3},{2,0},{3,1},{4,6},{5,7},{6,4},{7,5},{8,10},{9,11},{10,... | collective-permute-start | bytes 1032200 | tf_op jit(solution)/shard_map/ppermute | solution.py:39
  340.1 13.5 %collective-permute-start.32 = (bf16[128,1792]{1,0:T(8,128)(2,1)S(1)}, bf16[128,1792]{1,0:T(8,128)(2,1)S(1)}, u32[]{:S(2)}, u32[]{:S(2)}) collective-permute-start(bf16[128,1792]{1,0:T(8,128)(2,1)S(1)} %multiply_convert_fusion), channel_id=1, source_target_pairs={{0,4},{4,0},{8,12},{12,8},{16,20},{20,16},{24,28},{28,24},{1,5},{5... | collective-permute-start | bytes 1376264 | tf_op jit(solution)/shard_map/ppermute | solution.py:30
  342.8 18.5 %collective-permute-start.41 = (bf16[128,1792]{1,0:T(8,128)(2,1)S(1)}, bf16[128,1792]{1,0:T(8,128)(2,1)S(1)}, u32[]{:S(2)}, u32[]{:S(2)}) collective-permute-start(bf16[128,1792]{1,0:T(8,128)(2,1)S(1)} %fusion.24), channel_id=1, source_target_pairs={{0,4},{4,0},{8,12},{12,8},{16,20},{20,16},{24,28},{28,24},{1,5},{5... | collective-permute-start | bytes 1376264 | tf_op jit(solution)/shard_map/ppermute | solution.py:30
  (38 other events, 266.6 us)

commit v2 on v1

v2 whole, which is shorter than its diff:
```python
import functools

import jax
import jax.numpy as jnp
from jax import lax
from jax.experimental import pallas as pl
from jax.experimental.pallas import tpu as pltpu
from jax.sharding import PartitionSpec as P

BF = jnp.bfloat16
F32 = jnp.float32


def routing(routes, gate_weights, groups):
    onehot = routes[:, :, None] == jnp.arange(groups, dtype=jnp.int32)
    weight = jnp.sum(jnp.where(onehot, gate_weights[:, :, None], 0.0), axis=1).T
    picked = jnp.any(onehot, axis=1).T
    rows = routes.shape[0]
    before = jnp.arange(rows)[:, None] < jnp.arange(rows)[None, :]
    slot = jnp.dot(picked.astype(BF), before.astype(BF), preferred_element_type=F32)
    return jnp.stack([jnp.where(picked, slot, -1.0), weight])


def expert_kernel(pieces, order, near, far, w_gate, w_up, w_down, give, keep, gate, up, hidden):
    k = pl.program_id(0)
    both = 2 * pieces

    def add(rows):
        gate_part = jnp.dot(rows[...], w_gate[...], preferred_element_type=F32)
        up_part = jnp.dot(rows[...], w_up[...], preferred_element_type=F32)
        gate[...] += gate_part
        up[...] += up_part

    @pl.when(k == 0)
    def _():
        gate[...] = jnp.zeros_like(gate)
        up[...] = jnp.zeros_like(up)

    @pl.when(k < pieces)
    def _():
        add(near)

    @pl.when((k >= pieces) & (k < both))
    def _():
        add(far)

    @pl.when(k == both - 1)
    def _():
        v = gate[...]
        hidden[...] = (v / (1.0 + jnp.exp(-v)) * up[...]).astype(BF)

    @pl.when((k >= both) & (k < both + pieces))
    def _():
        give[...] = jnp.dot(hidden[...], w_down[...], preferred_element_type=F32).astype(BF)

    @pl.when(k >= both + pieces)
    def _():
        keep[...] = jnp.dot(hidden[...], w_down[...], preferred_element_type=F32).astype(BF)


def expert(order, near, far, w_gate, w_up, w_down, feats):
    rows, width = near.shape
    pieces = width // feats
    both = 2 * pieces
    units = w_down.shape[1]

    def at(low, high):
        return lambda k, order: (0, jnp.clip(k - low, 0, high - low - 1))

    grid = pltpu.PrefetchScalarGridSpec(
        num_scalar_prefetch=1,
        grid=(2 * both,),
        in_specs=[
            pl.BlockSpec((rows, feats), at(0, pieces)),
            pl.BlockSpec((rows, feats), at(pieces, both)),
            pl.BlockSpec((None, feats, units), lambda k, order: (0, order[jnp.minimum(k, both - 1)], 0)),
            pl.BlockSpec((None, feats, units), lambda k, order: (0, order[jnp.minimum(k, both - 1)], 0)),
            pl.BlockSpec((None, units, feats), lambda k, order: (0, 0, order[jnp.maximum(k, both)])),
        ],
        out_specs=[
            pl.BlockSpec((rows, feats), at(both, both + pieces)),
            pl.BlockSpec((rows, feats), at(both + pieces, 2 * both)),
        ],
        scratch_shapes=[
            pltpu.VMEM((rows, units), F32),
            pltpu.VMEM((rows, units), F32),
            pltpu.VMEM((rows, units), BF),
        ],
    )
    depth = w_gate.shape[1]
    return pl.pallas_call(
        functools.partial(expert_kernel, pieces),
        grid_spec=grid,
        out_shape=[jax.ShapeDtypeStruct((rows, width), BF)] * 2,
        compiler_params=pltpu.CompilerParams(vmem_limit_bytes=28 * 2**20),
        cost_estimate=pl.CostEstimate(
            flops=6 * rows * depth * units,
            bytes_accessed=6 * depth * units + 8 * rows * width,
            transcendentals=rows * units,
        ),
    )(order, near, far, w_gate, w_up, w_down)


def local(tokens, routes, gate_weights, w_gate, w_up, w_down):
    groups, inners = lax.axis_size("group"), lax.axis_size("inner")
    g, i = lax.axis_index("group"), lax.axis_index("inner")
    chips, planes = inners // 2, groups // 2
    x, c = i // 2, i % 2
    rows, feats = tokens.shape
    cap = rows * routes.shape[1] * 3 // (2 * groups)

    def over_y(a):
        return lax.ppermute(a, "group", [(j, j ^ 1) for j in range(groups)])

    def over_z(a):
        return lax.ppermute(a, "group", [(j, (j + 2) % groups) for j in range(groups)])

    def over_core(a):
        return lax.ppermute(a, "inner", [(j, j ^ 1) for j in range(inners)])

    def over_x(a, s):
        return lax.ppermute(a, "inner", [(j, (j + 2 * s) % inners) for j in range(inners)])

    came = [(x - s) % chips * 2 for s in range(chips)]
    goes = [(x + s) % chips * 2 for s in range(chips)]
    order = jnp.stack(
        [k + c for k in came] + [k + 1 - c for k in came] + [k + 1 - c for k in goes] + [k + c for k in goes]
    ).astype(jnp.int32)

    info = routing(routes, gate_weights, groups)
    infos = [jnp.stack([info, over_y(info)])]
    main = [tokens]
    for t in range(1, planes):
        infos.append(over_z(infos[-1]))
        main.append(over_z(main[-1]))
    other = [over_y(a) for a in main]

    slots = jnp.arange(cap, dtype=jnp.int32).astype(F32)
    q = []
    for t in range(planes):
        mine = lax.dynamic_index_in_dim(infos[t], g, 2, keepdims=False)
        blocks = []
        for u, block in enumerate((main[t], other[t])):
            placing = (mine[u, 0][None, :] == slots[:, None]).astype(BF)
            p = jnp.dot(placing, block, preferred_element_type=F32).astype(BF)
            blocks.append([p] + [over_x(p, s) for s in range(1, chips)])
        near = jnp.block(blocks)
        give, keep = expert(order, near, over_core(near), w_gate, w_up, w_down, feats)
        pair = keep.astype(F32) + over_core(give).astype(F32)
        weighted = []
        for u in (0, 1):
            here = pair[u * cap:(u + 1) * cap]
            total = here[:, :feats]
            for s in range(1, chips):
                total = total + over_x(here[:, s * feats:(s + 1) * feats].astype(BF), s).astype(F32)
            back = (mine[u, 0][:, None] == slots[None, :]).astype(BF)
            spread = jnp.dot(back, total.astype(BF), preferred_element_type=F32)
            weighted.append(spread * mine[u, 1][:, None])
        q.append(weighted[0] + over_y(weighted[1].astype(BF)).astype(F32))

    total = q[1 % planes]
    for t in range(2, planes + 1):
        total = over_z(total.astype(BF)).astype(F32) + q[t % planes]
    return total.astype(BF)


def solution(mesh):
    placed = (
        P("group", "inner"),
        P("group", None),
        P("group", None),
        P("group", None, "inner"),
        P("group", None, "inner"),
        P("group", "inner", None),
    )
    return jax.shard_map(
        local, mesh=mesh, in_specs=placed, out_specs=P("group", "inner"), check_vma=False
    )
```

time: 368 us -> 208 us (0.57)
  local copies, waits for them, and re-layouts: 124 us -> 0.32 us
  matrix products: 70.8 us -> 6.93 us
  Pallas kernels: 0 us -> 42.6 us
  other arithmetic: 23.1 us -> 4.05 us
  waiting for transfers between devices: 104 us -> 122 us
  starting transfers between devices: 42.5 us -> 30.8 us
    reshape x8 -> x0, local copies, waits for them, and re-layouts: 69.3 us -> none  [the longest x4 39.5 us: local(): full = jnp.stack([even, odd], axis=2).reshape(2 * cap, depth)]
    dot_general x8 -> x0, matrix products: 63.9 us -> none  [the longest x4 41.9 us: local(): part = jnp.dot(hidden, w_down[0], preferred_element_type=F32).astype(BF)]
    pallas_call x0 -> x4, Pallas kernels: none -> 42.6 us  [expert(): pl.pallas_call(functools.partial(expert_kernel, pieces), grid_spec=grid,...]
    slice x8 -> x4, local copies, waits for them, and re-layouts: 30.7 us -> 0.19 us  [local(): here[:, s * feats:(s + 1) * feats].astype(BF)]
    another operation x4 -> x1, local copies, waits for them, and re-layouts: 17.5 us -> 0.08 us  [local(): jnp.stack([k + c for k in came] + [k + 1 - c for k in came] + [k + 1 - c...]
    ppermute x16, waiting for transfers between devices: 61.6 us -> 72.1 us  [over_x(): lax.ppermute(a, 'inner', [(j, (j + 2 * s) % inners) for j in range(inners)])]
    another operation x12 -> x4, other arithmetic: 9.8 us -> 1.76 us  [the longest x8 5.77 us: local(): full = jnp.stack([even, odd], axis=2).reshape(2 * cap, depth)]
    ppermute x16, starting transfers between devices: 23.3 us -> 16 us  [over_x(): lax.ppermute(a, 'inner', [(j, (j + 2 * s) % inners) for j in range(inners)])]
  transfers between devices with their start and end apart: 42 -> 42, of which waited for: 20 -> 23; matrix products, arithmetic and copies ran while one was open for 58% -> 5% of each run, Pallas kernels for 0% -> 21%
where the time goes in v2:
time: 208 us; the launch traced here: 207 us
  waiting for transfers between devices  122 us (59%)
  Pallas kernels  42.6 us (20%)
  starting transfers between devices  30.8 us (15%)
  matrix products  6.93 us (3%)
  other arithmetic  4.05 us (2%)
    ppermute x16, waiting for transfers between devices, over_x(): lax.ppermute(a, 'inner', [(j, (j + 2 * s) % inners) for j in range(inners)])  72.1 us
    pallas_call x4, Pallas kernels, expert(): pl.pallas_call(functools.partial(expert_kernel, pieces), grid_spec=grid,...  42.6 us
    ppermute x9, waiting for transfers between devices, over_y(): return lax.ppermute(a, 'group', [(j, j ^ 1) for j in range(groups)])  28 us
    ppermute x9, waiting for transfers between devices, over_z(): lax.ppermute(a, 'group', [(j, (j + 2) % groups) for j in range(groups)])  21.8 us
    ppermute x16, starting transfers between devices, over_x(): lax.ppermute(a, 'inner', [(j, (j + 2 * s) % inners) for j in range(inners)])  16 us
    ppermute x9, starting transfers between devices, over_y(): return lax.ppermute(a, 'group', [(j, j ^ 1) for j in range(groups)])  7.89 us
    ppermute x9, starting transfers between devices, over_z(): lax.ppermute(a, 'group', [(j, (j + 2) % groups) for j in range(groups)])  5.29 us
  transfers between devices with their start and end apart: 42, of which 23 were waited for; matrix products, arithmetic and copies ran while one was open for 5% of the time, Pallas kernels for 21%

profile of v2, /device:TPU:0, one launch (start us, length us, event | category | flops | bytes accessed | tf_op | source)
XLA Modules:
  0.0 207.0 jit_solution(9899882611460337412)
XLA Ops:
  0.0 3.0 %collective-permute-start.2 = (bf16[128,1792]{1,0:T(8,128)(2,1)}, bf16[128,1792]{1,0:T(8,128)(2,1)S(1)}, u32[]{:S(2)}, u32[]{:S(2)}) collective-permute-start(bf16[128,1792]{1,0:T(8,128)(2,1)} %param.6), channel_id=1, source_target_pairs={{0,8},{4,12},{8,16},{12,20},{16,24},{20,28},{24,0},{28,4},{1,9},{5... | collective-permute-start | bytes 1376264 | tf_op jit(solution)/shard_map/ppermute | solution.py:116
  6.7 8.7 %collective-permute-done = f32[2,8,128]{2,1,0:T(8,128)S(1)} collective-permute-done((f32[2,8,128]{2,1,0:T(8,128)S(1)}, f32[2,8,128]{2,1,0:T(8,128)S(1)}, u32[]{:S(2)}, u32[]{:S(2)}) %collective-permute-start) | collective-permute-done | bytes 8224 | tf_op jit(solution)/shard_map/ppermute | solution.py:113
  21.5 5.0 %collective-permute-done.12 = f32[2,2,8,128]{3,2,1,0:T(8,128)S(1)} collective-permute-done((f32[2,2,8,128]{3,2,1,0:T(8,128)S(1)}, f32[2,2,8,128]{3,2,1,0:T(8,128)S(1)}, u32[]{:S(2)}, u32[]{:S(2)}) %collective-permute-start.12) | collective-permute-done | bytes 16416 | tf_op jit(solution)/shard_map/ppermute | solution.py:116
  26.5 5.5 %collective-permute-done.23 = f32[2,2,8,128]{3,2,1,0:T(8,128)S(1)} collective-permute-done((f32[2,2,8,128]{3,2,1,0:T(8,128)S(1)}, f32[2,2,8,128]{3,2,1,0:T(8,128)S(1)}, u32[]{:S(2)}, u32[]{:S(2)}) %collective-permute-start.23) | collective-permute-done | bytes 16416 | tf_op jit(solution)/shard_map/ppermute | solution.py:116
  36.4 4.2 %collective-permute-done.4 = bf16[128,1792]{1,0:T(8,128)(2,1)S(1)} collective-permute-done((bf16[128,1792]{1,0:T(8,128)(2,1)S(1)}, bf16[128,1792]{1,0:T(8,128)(2,1)S(1)}, u32[]{:S(2)}, u32[]{:S(2)}) %collective-permute-start.4) | collective-permute-done | bytes 458784 | tf_op jit(solution)/shard_map/ppermute | solution.py:113
  48.5 2.6 %collective-permute-done.3 = bf16[96,1792]{1,0:T(8,128)(2,1)S(1)} collective-permute-done((bf16[96,1792]{1,0:T(8,128)(2,1)S(1)}, bf16[96,1792]{1,0:T(8,128)(2,1)S(1)}, u32[]{:S(2)}, u32[]{:S(2)}) %collective-permute-start.3) | collective-permute-done | bytes 344096 | tf_op jit(solution)/shard_map/ppermute | solution.py:122
  51.7 5.6 %collective-permute-done.5 = bf16[96,1792]{1,0:T(8,128)(2,1)S(1)} collective-permute-done((bf16[96,1792]{1,0:T(8,128)(2,1)S(1)}, bf16[96,1792]{1,0:T(8,128)(2,1)S(1)}, u32[]{:S(2)}, u32[]{:S(2)}) %collective-permute-start.5) | collective-permute-done | bytes 344096 | tf_op jit(solution)/shard_map/ppermute | solution.py:122
  57.5 4.0 %collective-permute-done.24 = bf16[128,1792]{1,0:T(8,128)(2,1)S(1)} collective-permute-done((bf16[128,1792]{1,0:T(8,128)(2,1)S(1)}, bf16[128,1792]{1,0:T(8,128)(2,1)S(1)}, u32[]{:S(2)}, u32[]{:S(2)}) %collective-permute-start.24) | collective-permute-done | bytes 458784 | tf_op jit(solution)/shard_map/ppermute | solution.py:116
  63.2 8.5 %collective-permute-done.26 = bf16[128,1792]{1,0:T(8,128)(2,1)S(1)} collective-permute-done((bf16[128,1792]{1,0:T(8,128)(2,1)S(1)}, bf16[128,1792]{1,0:T(8,128)(2,1)S(1)}, u32[]{:S(2)}, u32[]{:S(2)}) %collective-permute-start.26) | collective-permute-done | bytes 458784 | tf_op jit(solution)/shard_map/ppermute | solution.py:113
  74.3 8.0 %collective-permute-done.25 = bf16[96,1792]{1,0:T(8,128)(2,1)S(1)} collective-permute-done((bf16[96,1792]{1,0:T(8,128)(2,1)S(1)}, bf16[96,1792]{1,0:T(8,128)(2,1)S(1)}, u32[]{:S(2)}, u32[]{:S(2)}) %collective-permute-start.25) | collective-permute-done | bytes 344096 | tf_op jit(solution)/shard_map/ppermute | solution.py:122
  82.2 3.7 %collective-permute-done.27 = bf16[96,1792]{1,0:T(8,128)(2,1)S(1)} collective-permute-done((bf16[96,1792]{1,0:T(8,128)(2,1)S(1)}, bf16[96,1792]{1,0:T(8,128)(2,1)S(1)}, u32[]{:S(2)}, u32[]{:S(2)}) %collective-permute-start.27) | collective-permute-done | bytes 344096 | tf_op jit(solution)/shard_map/ppermute | solution.py:122
  86.1 10.6 %shard_map.67 = (bf16[192,3584]{1,0:T(8,128)(2,1)S(1)}, bf16[192,3584]{1,0:T(8,128)(2,1)S(1)}) custom-call(s32[8]{0:T(128)S(1)} %stack.53.order, bf16[192,3584]{1,0:T(8,128)(2,1)S(1)} %maximum_maximum_fusion.3.near, bf16[192,3584]{1,0:T(8,128)(2,1)S(1)} %collective-permute-done.37.far, bf16[1,7168,512]{2,1,0:T(8,128)(2,1)S(1)} %bitcast.62, ...), custom_call_target="tpu_custom_call" | custom-call | flops 4227858432 | bytes 27525120 | tf_op jit(solution)/shard_map/pallas_call | solution.py:91
  97.3 10.6 %shard_map.64 = (bf16[192,3584]{1,0:T(8,128)(2,1)S(1)}, bf16[192,3584]{1,0:T(8,128)(2,1)S(1)}) custom-call(s32[8]{0:T(128)S(1)} %stack.53.order, bf16[192,3584]{1,0:T(8,128)(2,1)S(1)} %maximum_maximum_fusion.near, bf16[192,3584]{1,0:T(8,128)(2,1)S(1)} %collective-permute-done.6.far, bf16[1,7168,512]{2,1,0:T(8,128)(2,1)S(1)} %bitcast.62, ...), custom_call_target="tpu_custom_call" | custom-call | flops 4227858432 | bytes 27525120 | tf_op jit(solution)/shard_map/pallas_call | solution.py:91
  108.0 10.6 %shard_map.65 = (bf16[192,3584]{1,0:T(8,128)(2,1)S(1)}, bf16[192,3584]{1,0:T(8,128)(2,1)S(1)}) custom-call(s32[8]{0:T(128)S(1)} %stack.53.order, bf16[192,3584]{1,0:T(8,128)(2,1)S(1)} %maximum_maximum_fusion.1.near, bf16[192,3584]{1,0:T(8,128)(2,1)S(1)} %collective-permute-done.17.far, bf16[1,7168,512]{2,1,0:T(8,128)(2,1)S(1)} %bitcast.62, ...), custom_call_target="tpu_custom_call" | custom-call | flops 4227858432 | bytes 27525120 | tf_op jit(solution)/shard_map/pallas_call | solution.py:91
  119.2 10.8 %shard_map.66 = (bf16[192,3584]{1,0:T(8,128)(2,1)S(1)}, bf16[192,3584]{1,0:T(8,128)(2,1)S(1)}) custom-call(s32[8]{0:T(128)S(1)} %stack.53.order, bf16[192,3584]{1,0:T(8,128)(2,1)S(1)} %maximum_maximum_fusion.2.near, bf16[192,3584]{1,0:T(8,128)(2,1)S(1)} %collective-permute-done.28.far, bf16[1,7168,512]{2,1,0:T(8,128)(2,1)S(1)} %bitcast.62, ...), custom_call_target="tpu_custom_call" | custom-call | flops 4227858432 | bytes 27525120 | tf_op jit(solution)/shard_map/pallas_call | solution.py:91
  135.8 6.1 %collective-permute-done.9 = bf16[96,1792]{1,0:T(8,128)(2,1)S(1)} collective-permute-done((bf16[96,1792]{1,0:T(8,128)(2,1)S(1)}, bf16[96,1792]{1,0:T(8,128)(2,1)S(1)}, u32[]{:S(2)}, u32[]{:S(2)}) %collective-permute-start.9) | collective-permute-done | bytes 344096 | tf_op jit(solution)/shard_map/ppermute | solution.py:122
  142.9 6.5 %collective-permute-done.20 = bf16[96,1792]{1,0:T(8,128)(2,1)S(1)} collective-permute-done((bf16[96,1792]{1,0:T(8,128)(2,1)S(1)}, bf16[96,1792]{1,0:T(8,128)(2,1)S(1)}, u32[]{:S(2)}, u32[]{:S(2)}) %collective-permute-start.20) | collective-permute-done | bytes 344096 | tf_op jit(solution)/shard_map/ppermute | solution.py:122
  151.3 12.8 %collective-permute-done.8 = bf16[96,1792]{1,0:T(8,128)(2,1)S(1)} collective-permute-done((bf16[96,1792]{1,0:T(8,128)(2,1)S(1)}, bf16[96,1792]{1,0:T(8,128)(2,1)S(1)}, u32[]{:S(2)}, u32[]{:S(2)}) %collective-permute-start.8) | collective-permute-done | bytes 344096 | tf_op jit(solution)/shard_map/ppermute | solution.py:122
  165.0 6.5 %collective-permute-done.19 = bf16[96,1792]{1,0:T(8,128)(2,1)S(1)} collective-permute-done((bf16[96,1792]{1,0:T(8,128)(2,1)S(1)}, bf16[96,1792]{1,0:T(8,128)(2,1)S(1)}, u32[]{:S(2)}, u32[]{:S(2)}) %collective-permute-start.19) | collective-permute-done | bytes 344096 | tf_op jit(solution)/shard_map/ppermute | solution.py:122
  172.4 6.5 %collective-permute-done.31 = bf16[96,1792]{1,0:T(8,128)(2,1)S(1)} collective-permute-done((bf16[96,1792]{1,0:T(8,128)(2,1)S(1)}, bf16[96,1792]{1,0:T(8,128)(2,1)S(1)}, u32[]{:S(2)}, u32[]{:S(2)}) %collective-permute-start.31) | collective-permute-done | bytes 344096 | tf_op jit(solution)/shard_map/ppermute | solution.py:122
  182.0 3.8 %collective-permute-done.30 = bf16[96,1792]{1,0:T(8,128)(2,1)S(1)} collective-permute-done((bf16[96,1792]{1,0:T(8,128)(2,1)S(1)}, bf16[96,1792]{1,0:T(8,128)(2,1)S(1)}, u32[]{:S(2)}, u32[]{:S(2)}) %collective-permute-start.30) | collective-permute-done | bytes 344096 | tf_op jit(solution)/shard_map/ppermute | solution.py:122
  186.1 6.6 %collective-permute-done.32 = bf16[128,1792]{1,0:T(8,128)(2,1)S(1)} collective-permute-done((bf16[128,1792]{1,0:T(8,128)(2,1)S(1)}, bf16[128,1792]{1,0:T(8,128)(2,1)S(1)}, u32[]{:S(2)}, u32[]{:S(2)}) %collective-permute-start.32) | collective-permute-done | bytes 458784 | tf_op jit(solution)/shard_map/ppermute | solution.py:113
  194.2 7.5 %collective-permute-done.39 = bf16[96,1792]{1,0:T(8,128)(2,1)S(1)} collective-permute-done((bf16[96,1792]{1,0:T(8,128)(2,1)S(1)}, bf16[96,1792]{1,0:T(8,128)(2,1)S(1)}, u32[]{:S(2)}, u32[]{:S(2)}) %collective-permute-start.39) | collective-permute-done | bytes 344096 | tf_op jit(solution)/shard_map/ppermute | solution.py:122
  201.7 4.2 %collective-permute-done.33 = bf16[128,1792]{1,0:T(8,128)(2,1)S(1)} collective-permute-done((bf16[128,1792]{1,0:T(8,128)(2,1)S(1)}, bf16[128,1792]{1,0:T(8,128)(2,1)S(1)}, u32[]{:S(2)}, u32[]{:S(2)}) %collective-permute-start.33) | collective-permute-done | bytes 458784 | tf_op jit(solution)/shard_map/ppermute | solution.py:116
  (116 shorter events, 44.8 us)
Async XLA Ops:
  0.0 32.0 %collective-permute-start.2 = (bf16[128,1792]{1,0:T(8,128)(2,1)}, bf16[128,1792]{1,0:T(8,128)(2,1)S(1)}, u32[]{:S(2)}, u32[]{:S(2)}) collective-permute-start(bf16[128,1792]{1,0:T(8,128)(2,1)} %param.6), channel_id=1, source_target_pairs={{0,8},{4,12},{8,16},{12,20},{16,24},{20,28},{24,0},{28,4},{1,9},{5... | collective-permute-start | bytes 1376264 | tf_op jit(solution)/shard_map/ppermute | solution.py:116
  3.0 30.6 %collective-permute-start.35 = (bf16[128,1792]{1,0:T(8,128)(2,1)}, bf16[128,1792]{1,0:T(8,128)(2,1)S(1)}, u32[]{:S(2)}, u32[]{:S(2)}) collective-permute-start(bf16[128,1792]{1,0:T(8,128)(2,1)} %param.6), channel_id=1, source_target_pairs={{0,4},{4,0},{8,12},{12,8},{16,20},{20,16},{24,28},{28,24},{1,5},{5... | collective-permute-start | bytes 1376264 | tf_op jit(solution)/shard_map/ppermute | solution.py:113
  18.3 24.1 %collective-permute-start.34 = (bf16[96,1792]{1,0:T(8,128)(2,1)S(1)}, bf16[96,1792]{1,0:T(8,128)(2,1)S(1)}, u32[]{:S(2)}, u32[]{:S(2)}) collective-permute-start(bf16[96,1792]{1,0:T(8,128)(2,1)S(1)} %convolution_convert_fusion.1), channel_id=1, source_target_pairs={{0,2},{1,3},{2,0},{3,1},{4,6},{5,7},{6,4},{7,5},{8,10},{9,11},{10,... | collective-permute-start | bytes 1032200 | tf_op jit(solution)/shard_map/ppermute | solution.py:122
  35.8 15.4 %collective-permute-start.3 = (bf16[96,1792]{1,0:T(8,128)(2,1)S(1)}, bf16[96,1792]{1,0:T(8,128)(2,1)S(1)}, u32[]{:S(2)}, u32[]{:S(2)}) collective-permute-start(bf16[96,1792]{1,0:T(8,128)(2,1)S(1)} %convolution_convert_fusion.7), channel_id=1, source_target_pairs={{0,2},{1,3},{2,0},{3,1},{4,6},{5,7},{6,4},{7,5},{8,10},{9,11},{10,... | collective-permute-start | bytes 1032200 | tf_op jit(solution)/shard_map/ppermute | solution.py:122
  40.9 16.4 %collective-permute-start.5 = (bf16[96,1792]{1,0:T(8,128)(2,1)S(1)}, bf16[96,1792]{1,0:T(8,128)(2,1)S(1)}, u32[]{:S(2)}, u32[]{:S(2)}) collective-permute-start(bf16[96,1792]{1,0:T(8,128)(2,1)S(1)} %convolution_convert_fusion.6), channel_id=1, source_target_pairs={{0,2},{1,3},{2,0},{3,1},{4,6},{5,7},{6,4},{7,5},{8,10},{9,11},{10,... | collective-permute-start | bytes 1032200 | tf_op jit(solution)/shard_map/ppermute | solution.py:122
  45.1 41.0 %collective-permute-start.37 = (bf16[192,3584]{1,0:T(8,128)(2,1)S(1)}, bf16[192,3584]{1,0:T(8,128)(2,1)S(1)}, u32[]{:S(2)}, u32[]{:S(2)}) collective-permute-start(bf16[192,3584]{1,0:T(8,128)(2,1)S(1)} %maximum_maximum_fusion.3.near), channel_id=1, source_target_pairs={{0,1},{1,0},{2,3},{3,2},{4,5},{5,4},{6,7},{7,6},{8,9},{9,8},{10,11... | collective-permute-start | bytes 4128776 | tf_op jit(solution)/shard_map/ppermute | solution.py:119
  47.0 25.6 %collective-permute-start.14 = (bf16[96,1792]{1,0:T(8,128)(2,1)S(1)}, bf16[96,1792]{1,0:T(8,128)(2,1)S(1)}, u32[]{:S(2)}, u32[]{:S(2)}) collective-permute-start(bf16[96,1792]{1,0:T(8,128)(2,1)S(1)} %convolution_convert_fusion.5), channel_id=1, source_target_pairs={{0,2},{1,3},{2,0},{3,1},{4,6},{5,7},{6,4},{7,5},{8,10},{9,11},{10,... | collective-permute-start | bytes 1032200 | tf_op jit(solution)/shard_map/ppermute | solution.py:122
  57.4 39.9 %collective-permute-start.6 = (bf16[192,3584]{1,0:T(8,128)(2,1)S(1)}, bf16[192,3584]{1,0:T(8,128)(2,1)S(1)}, u32[]{:S(2)}, u32[]{:S(2)}) collective-permute-start(bf16[192,3584]{1,0:T(8,128)(2,1)S(1)} %maximum_maximum_fusion.near), channel_id=1, source_target_pairs={{0,1},{1,0},{2,3},{3,2},{4,5},{5,4},{6,7},{7,6},{8,9},{9,8},{10,11... | collective-permute-start | bytes 4128776 | tf_op jit(solution)/shard_map/ppermute | solution.py:119
  74.2 33.8 %collective-permute-start.17 = (bf16[192,3584]{1,0:T(8,128)(2,1)S(1)}, bf16[192,3584]{1,0:T(8,128)(2,1)S(1)}, u32[]{:S(2)}, u32[]{:S(2)}) collective-permute-start(bf16[192,3584]{1,0:T(8,128)(2,1)S(1)} %maximum_maximum_fusion.1.near), channel_id=1, source_target_pairs={{0,1},{1,0},{2,3},{3,2},{4,5},{5,4},{6,7},{7,6},{8,9},{9,8},{10,11... | collective-permute-start | bytes 4128776 | tf_op jit(solution)/shard_map/ppermute | solution.py:119
  86.0 33.1 %collective-permute-start.28 = (bf16[192,3584]{1,0:T(8,128)(2,1)S(1)}, bf16[192,3584]{1,0:T(8,128)(2,1)S(1)}, u32[]{:S(2)}, u32[]{:S(2)}) collective-permute-start(bf16[192,3584]{1,0:T(8,128)(2,1)S(1)} %maximum_maximum_fusion.2.near), channel_id=1, source_target_pairs={{0,1},{1,0},{2,3},{3,2},{4,5},{5,4},{6,7},{7,6},{8,9},{9,8},{10,11... | collective-permute-start | bytes 4128776 | tf_op jit(solution)/shard_map/ppermute | solution.py:119
  96.7 33.3 %collective-permute-start.38 = (bf16[192,3584]{1,0:T(8,128)(2,1)S(1)}, bf16[192,3584]{1,0:T(8,128)(2,1)S(1)}, u32[]{:S(2)}, u32[]{:S(2)}) collective-permute-start(bf16[192,3584]{1,0:T(8,128)(2,1)S(1)} %get-tuple-element.20), channel_id=1, source_target_pairs={{0,1},{1,0},{2,3},{3,2},{4,5},{5,4},{6,7},{7,6},{8,9},{9,8},{10,11... | collective-permute-start | bytes 4128776 | tf_op jit(solution)/shard_map/ppermute | solution.py:119
  107.9 22.6 %collective-permute-start.7 = (bf16[192,3584]{1,0:T(8,128)(2,1)S(1)}, bf16[192,3584]{1,0:T(8,128)(2,1)S(1)}, u32[]{:S(2)}, u32[]{:S(2)}) collective-permute-start(bf16[192,3584]{1,0:T(8,128)(2,1)S(1)} %get-tuple-element.14), channel_id=1, source_target_pairs={{0,1},{1,0},{2,3},{3,2},{4,5},{5,4},{6,7},{7,6},{8,9},{9,8},{10,11... | collective-permute-start | bytes 4128776 | tf_op jit(solution)/shard_map/ppermute | solution.py:119
  130.0 20.2 %collective-permute-start.29 = (bf16[192,3584]{1,0:T(8,128)(2,1)S(1)}, bf16[192,3584]{1,0:T(8,128)(2,1)S(1)}, u32[]{:S(2)}, u32[]{:S(2)}) collective-permute-start(bf16[192,3584]{1,0:T(8,128)(2,1)S(1)} %get-tuple-element.18), channel_id=1, source_target_pairs={{0,1},{1,0},{2,3},{3,2},{4,5},{5,4},{6,7},{7,6},{8,9},{9,8},{10,11... | collective-permute-start | bytes 4128776 | tf_op jit(solution)/shard_map/ppermute | solution.py:119
  132.1 17.2 %collective-permute-start.20 = (bf16[96,1792]{1,0:T(8,128)(2,1)S(1)}, bf16[96,1792]{1,0:T(8,128)(2,1)S(1)}, u32[]{:S(2)}, u32[]{:S(2)}) collective-permute-start(bf16[96,1792]{1,0:T(8,128)(2,1)S(1)} %get-tuple-element.34), channel_id=1, source_target_pairs={{0,2},{1,3},{2,0},{3,1},{4,6},{5,7},{6,4},{7,5},{8,10},{9,11},{10,... | collective-permute-start | bytes 1032200 | tf_op jit(solution)/shard_map/ppermute | solution.py:122
  133.8 46.3 %collective-permute-start.40 = (bf16[96,1792]{1,0:T(8,128)(2,1)S(1)}, bf16[96,1792]{1,0:T(8,128)(2,1)S(1)}, u32[]{:S(2)}, u32[]{:S(2)}) collective-permute-start(bf16[96,1792]{1,0:T(8,128)(2,1)S(1)} %get-tuple-element.30), channel_id=1, source_target_pairs={{0,2},{1,3},{2,0},{3,1},{4,6},{5,7},{6,4},{7,5},{8,10},{9,11},{10,... | collective-permute-start | bytes 1032200 | tf_op jit(solution)/shard_map/ppermute | solution.py:122
  134.3 29.8 %collective-permute-start.8 = (bf16[96,1792]{1,0:T(8,128)(2,1)S(1)}, bf16[96,1792]{1,0:T(8,128)(2,1)S(1)}, u32[]{:S(2)}, u32[]{:S(2)}) collective-permute-start(bf16[96,1792]{1,0:T(8,128)(2,1)S(1)} %get-tuple-element.31), channel_id=1, source_target_pairs={{0,2},{1,3},{2,0},{3,1},{4,6},{5,7},{6,4},{7,5},{8,10},{9,11},{10,... | collective-permute-start | bytes 1032200 | tf_op jit(solution)/shard_map/ppermute | solution.py:122
  142.3 22.3 %collective-permute-start.10 = (bf16[128,1792]{1,0:T(8,128)(2,1)S(1)}, bf16[128,1792]{1,0:T(8,128)(2,1)S(1)}, u32[]{:S(2)}, u32[]{:S(2)}) collective-permute-start(bf16[128,1792]{1,0:T(8,128)(2,1)S(1)} %fusion.3), channel_id=1, source_target_pairs={{0,4},{4,0},{8,12},{12,8},{16,20},{20,16},{24,28},{28,24},{1,5},{5... | collective-permute-start | bytes 1376264 | tf_op jit(solution)/shard_map/ppermute | solution.py:113
  149.3 22.1 %collective-permute-start.19 = (bf16[96,1792]{1,0:T(8,128)(2,1)S(1)}, bf16[96,1792]{1,0:T(8,128)(2,1)S(1)}, u32[]{:S(2)}, u32[]{:S(2)}) collective-permute-start(bf16[96,1792]{1,0:T(8,128)(2,1)S(1)} %get-tuple-element.33), channel_id=1, source_target_pairs={{0,2},{1,3},{2,0},{3,1},{4,6},{5,7},{6,4},{7,5},{8,10},{9,11},{10,... | collective-permute-start | bytes 1032200 | tf_op jit(solution)/shard_map/ppermute | solution.py:122
  150.2 29.5 %collective-permute-start.21 = (bf16[128,1792]{1,0:T(8,128)(2,1)S(1)}, bf16[128,1792]{1,0:T(8,128)(2,1)S(1)}, u32[]{:S(2)}, u32[]{:S(2)}) collective-permute-start(bf16[128,1792]{1,0:T(8,128)(2,1)S(1)} %multiply_convert_fusion.1), channel_id=1, source_target_pairs={{0,4},{4,0},{8,12},{12,8},{16,20},{20,16},{24,28},{28,24},{1,5},{5... | collective-permute-start | bytes 1376264 | tf_op jit(solution)/shard_map/ppermute | solution.py:113
  164.1 14.7 %collective-permute-start.31 = (bf16[96,1792]{1,0:T(8,128)(2,1)S(1)}, bf16[96,1792]{1,0:T(8,128)(2,1)S(1)}, u32[]{:S(2)}, u32[]{:S(2)}) collective-permute-start(bf16[96,1792]{1,0:T(8,128)(2,1)S(1)} %get-tuple-element.36), channel_id=1, source_target_pairs={{0,2},{1,3},{2,0},{3,1},{4,6},{5,7},{6,4},{7,5},{8,10},{9,11},{10,... | collective-permute-start | bytes 1032200 | tf_op jit(solution)/shard_map/ppermute | solution.py:122
  164.9 14.8 %collective-permute-start.11 = (bf16[128,1792]{1,0:T(8,128)(2,1)S(1)}, bf16[128,1792]{1,0:T(8,128)(2,1)S(1)}, u32[]{:S(2)}, u32[]{:S(2)}) collective-permute-start(bf16[128,1792]{1,0:T(8,128)(2,1)S(1)} %fusion.2), channel_id=1, source_target_pairs={{0,8},{4,12},{8,16},{12,20},{16,24},{20,28},{24,0},{28,4},{1,9},{5... | collective-permute-start | bytes 1376264 | tf_op jit(solution)/shard_map/ppermute | solution.py:116
  171.8 14.0 %collective-permute-start.30 = (bf16[96,1792]{1,0:T(8,128)(2,1)S(1)}, bf16[96,1792]{1,0:T(8,128)(2,1)S(1)}, u32[]{:S(2)}, u32[]{:S(2)}) collective-permute-start(bf16[96,1792]{1,0:T(8,128)(2,1)S(1)} %get-tuple-element.35), channel_id=1, source_target_pairs={{0,2},{1,3},{2,0},{3,1},{4,6},{5,7},{6,4},{7,5},{8,10},{9,11},{10,... | collective-permute-start | bytes 1032200 | tf_op jit(solution)/shard_map/ppermute | solution.py:122
  179.2 13.5 %collective-permute-start.32 = (bf16[128,1792]{1,0:T(8,128)(2,1)S(1)}, bf16[128,1792]{1,0:T(8,128)(2,1)S(1)}, u32[]{:S(2)}, u32[]{:S(2)}) collective-permute-start(bf16[128,1792]{1,0:T(8,128)(2,1)S(1)} %multiply_convert_fusion), channel_id=1, source_target_pairs={{0,4},{4,0},{8,12},{12,8},{16,20},{20,16},{24,28},{28,24},{1,5},{5... | collective-permute-start | bytes 1376264 | tf_op jit(solution)/shard_map/ppermute | solution.py:113
  180.4 21.3 %collective-permute-start.41 = (bf16[128,1792]{1,0:T(8,128)(2,1)S(1)}, bf16[128,1792]{1,0:T(8,128)(2,1)S(1)}, u32[]{:S(2)}, u32[]{:S(2)}) collective-permute-start(bf16[128,1792]{1,0:T(8,128)(2,1)S(1)} %fusion.4), channel_id=1, source_target_pairs={{0,4},{4,0},{8,12},{12,8},{16,20},{20,16},{24,28},{28,24},{1,5},{5... | collective-permute-start | bytes 1376264 | tf_op jit(solution)/shard_map/ppermute | solution.py:113
  (21 other events, 281.7 us)

commit v3 on v1

v3 whole, which is shorter than its diff:
```python
import functools

import jax
import jax.numpy as jnp
from jax import lax
from jax.experimental import pallas as pl
from jax.experimental.pallas import tpu as pltpu
from jax.sharding import PartitionSpec as P

BF = jnp.bfloat16
F32 = jnp.float32
TOKEN = jax.ShapeDtypeStruct((8, 128), F32)
PACK, EXPERT, PAIR, SPREAD, LABEL = 10, 40, 0.7, 1.5, 1.0
VMEM_MIB, EXPERT_MIB = 12, 22


def behind(kernel, reads, after):
    return lambda *refs: kernel(*refs[:reads], *refs[reads + after:])


def call(kernel, out_shape, specs, operands, after, us, mib=VMEM_MIB):
    vmem = pl.BlockSpec(memory_space=pltpu.VMEM)
    return pl.pallas_call(
        behind(kernel, len(operands), len(after)),
        in_specs=[s or vmem for s in specs] + [pl.BlockSpec(memory_space=pl.ANY)] * len(after),
        out_specs=[vmem] * (len(out_shape) + 1),
        out_shape=[*out_shape, TOKEN],
        compiler_params=pltpu.CompilerParams(vmem_limit_bytes=mib * 2**20),
        cost_estimate=hint(us),
    )(*operands, *after)


def hint(us):
    return pl.CostEstimate(flops=int(us * 1e9), bytes_accessed=1024, transcendentals=0)


SMEM = pl.BlockSpec(memory_space=pltpu.SMEM)


def label_kernel(tokens, routes, weights, block, token):
    rows = tokens.shape[0]
    block[:rows, :] = tokens[...]
    w = weights[...]
    high = w.astype(BF).astype(F32)
    middle = (w - high).astype(BF).astype(F32)
    low = w - high - middle
    spare = block.shape[0] - rows - 4 * w.shape[0]
    parts = [routes[...].astype(F32), high, middle, low] + [jnp.zeros((spare, rows), F32)] * (spare > 0)
    block[rows:, :rows] = jnp.concatenate(parts, axis=0).astype(BF)
    if block.shape[1] > rows:
        block[rows:, rows:] = jnp.zeros((block.shape[0] - rows, block.shape[1] - rows), BF)
    token[...] = jnp.zeros_like(token)


def label(tokens, routes, gate_weights, after):
    rows, feats = tokens.shape
    extra = -(-4 * routes.shape[1] // 16) * 16
    out = [jax.ShapeDtypeStruct((rows + extra, feats), BF)]
    return call(label_kernel, out, [None] * 3, (tokens, routes.T, gate_weights.T), after, LABEL)


def placing_of(labels, me, cap, choices):
    rows = labels.shape[1]
    named = labels[:choices] == me.astype(F32)
    weights = labels[choices:2 * choices] + labels[2 * choices:3 * choices] + labels[3 * choices:4 * choices]
    weight = jnp.sum(jnp.where(named, weights, 0.0), axis=0, keepdims=True)
    picked = jnp.sum(jnp.where(named, 1.0, 0.0), axis=0, keepdims=True)
    one, two = (lax.broadcasted_iota(jnp.int32, (rows, rows), n) for n in (0, 1))
    before = jnp.where(one < two, 1.0, 0.0).astype(BF)
    many = jnp.broadcast_to(picked, (16, rows)).astype(BF)
    slot = jnp.dot(many, before, preferred_element_type=F32)[:1]
    slot = jnp.where(picked > 0.5, slot, -1.0).astype(jnp.int32)
    return lax.broadcasted_iota(jnp.int32, (cap, rows), 0) == slot, weight


def joined(pieces, near):
    feats = pieces[0].shape[1]
    for n, piece in enumerate(pieces):
        near[:, n * feats:(n + 1) * feats] = piece[...]


def join_kernel(*refs):
    *pieces, near, token = refs
    joined(pieces, near)
    token[...] = jnp.zeros_like(token)


def side_by_side(pieces):
    return [jax.ShapeDtypeStruct((pieces[0].shape[0], len(pieces) * pieces[0].shape[1]), BF)] if pieces else []


def join(pieces, after):
    return call(join_kernel, side_by_side(pieces), [None] * len(pieces), pieces, after, PACK)


def pack_kernel(choices, ahead, before, at, *refs):
    blocks, following, pieces = refs[:2], refs[2:2 + ahead], refs[2 + ahead:2 + ahead + before]
    packed, labels, *rest, token = refs[2 + ahead + before:]
    for a, b in zip(following, rest[:ahead], strict=True):
        b[...] = a[...]
    if before:
        joined(pieces, rest[ahead])
    rows, cap = labels.shape[2], packed.shape[0] // len(blocks)
    parts = []
    for u, block in enumerate(blocks):
        lines = block[rows:, :rows].astype(F32)
        labels[u] = lines
        placing, _ = placing_of(lines, at[0], cap, choices)
        placing = jnp.where(placing, 1.0, 0.0).astype(BF)
        parts.append(jnp.dot(placing, block[:rows, :], preferred_element_type=F32))
    packed[...] = jnp.concatenate(parts, axis=0).astype(BF)
    token[...] = jnp.zeros_like(token)


def pack(at, blocks, following, pieces, rows, choices, cap, after):
    n = len(blocks)
    shapes = [((n * cap, blocks[0].shape[1]), BF), ((n, blocks[0].shape[0] - rows, rows), F32)]
    out = [jax.ShapeDtypeStruct(*a) for a in shapes] + [jax.ShapeDtypeStruct(a.shape, BF) for a in following]
    kernel = functools.partial(pack_kernel, choices, len(following), len(pieces))
    operands = (at, *blocks, *following, *pieces)
    specs = [SMEM] + [None] * (len(operands) - 1)
    packed, labels, *rest, token = call(kernel, out + side_by_side(pieces), specs, operands, after, PACK)
    return packed, labels, rest[:len(following)], rest[len(following):], token


def pair_kernel(keep, rec, *refs):
    *outs, token = refs
    feats = outs[0].shape[1]
    for s, out in enumerate(outs):
        here = slice(s * feats, (s + 1) * feats)
        out[...] = (keep[:, here].astype(F32) + rec[:, here].astype(F32)).astype(out.dtype)
    token[...] = jnp.zeros_like(token)


def pair_sum(keep, rec, feats, after):
    rows, width = keep.shape
    out = [jax.ShapeDtypeStruct((rows, feats), BF if s else F32) for s in range(width // feats)]
    *outs, token = call(pair_kernel, out, [None] * 2, (keep, rec), after, PAIR)
    return outs, token


def spread_kernel(choices, at, labels, *refs):
    *terms, stay, go, token = refs
    total = terms[0][...].astype(F32)
    for a in terms[1:]:
        total = total + a[...].astype(F32)
    cap = total.shape[0] // 2
    across = (((0,), (0,)), ((), ()))
    for u, out in enumerate((stay, go)):
        here = total[u * cap:(u + 1) * cap].astype(BF)
        placing, weight = placing_of(labels[u], at[0], cap, choices)
        table = jnp.where(placing, weight, 0.0)
        high = table.astype(BF)
        low = (table - high.astype(F32)).astype(BF)
        value = lax.dot_general(high, here, across, preferred_element_type=F32)
        value += lax.dot_general(low, here, across, preferred_element_type=F32)
        out[...] = value.astype(out.dtype)
    token[...] = jnp.zeros_like(token)


def spread(at, labels, choices, terms, after):
    shape = (labels.shape[2], terms[0].shape[1])
    out = [jax.ShapeDtypeStruct(shape, F32), jax.ShapeDtypeStruct(shape, BF)]
    kernel = functools.partial(spread_kernel, choices)
    return call(kernel, out, [SMEM] + [None] * (1 + len(terms)), (at, labels, *terms), after, SPREAD)


def expert_kernel(half, order, near, far, w_gate, w_up, w_down, give, keep, token, gate, up, hidden):
    k = pl.program_id(0)
    both = 2 * half

    def first(rows):
        gate[...] += jnp.dot(rows[...], w_gate[...], preferred_element_type=F32)
        up[...] += jnp.dot(rows[...], w_up[...], preferred_element_type=F32)

    @pl.when(k == 0)
    def _():
        gate[...] = jnp.zeros_like(gate)
        up[...] = jnp.zeros_like(up)
        token[...] = jnp.zeros_like(token)

    pl.when(k < half)(functools.partial(first, near))
    pl.when((k >= half) & (k < both))(functools.partial(first, far))

    @pl.when(k == both - 1)
    def _():
        v = gate[...]
        hidden[...] = (v / (1.0 + jnp.exp(-v)) * up[...]).astype(BF)

    def second(out):
        out[...] = jnp.dot(hidden[...], w_down[...], preferred_element_type=F32).astype(BF)

    pl.when((k >= both) & (k < both + half))(functools.partial(second, give))
    pl.when(k >= both + half)(functools.partial(second, keep))


def expert(order, near, far, feats, w_gate, w_up, w_down, after):
    rows, width = near.shape
    units = w_gate.shape[2]
    half = width // feats
    both = 2 * half
    into = pl.BlockSpec((None, feats, units), lambda k, order: (0, order[jnp.minimum(k, both - 1)], 0))

    def part(first):
        return pl.BlockSpec((rows, feats), lambda k, order: (0, jnp.clip(k - first, 0, half - 1)))

    grid = pltpu.PrefetchScalarGridSpec(
        num_scalar_prefetch=1,
        grid=(2 * both,),
        in_specs=[part(0), part(half), into, into]
        + [pl.BlockSpec((None, units, feats), lambda k, order: (0, 0, order[jnp.maximum(k, both)]))]
        + [pl.BlockSpec(memory_space=pl.ANY)] * len(after),
        out_specs=[part(both), part(both + half), pl.BlockSpec((8, 128), lambda k, order: (0, 0))],
        scratch_shapes=[pltpu.VMEM((rows, units), F32)] * 2 + [pltpu.VMEM((rows, units), BF)],
    )
    return pl.pallas_call(
        behind(functools.partial(expert_kernel, half), 6, len(after)),
        grid_spec=grid,
        out_shape=[jax.ShapeDtypeStruct((rows, width), BF)] * 2 + [TOKEN],
        compiler_params=pltpu.CompilerParams(vmem_limit_bytes=EXPERT_MIB * 2**20),
        cost_estimate=hint(EXPERT),
    )(order, near, far, w_gate, w_up, w_down, *after)


def local(tokens, routes, gate_weights, w_gate, w_up, w_down):
    groups, inners = lax.axis_size("group"), lax.axis_size("inner")
    g, i = lax.axis_index("group"), lax.axis_index("inner")
    chips, planes = inners // 2, groups // 2
    x, c = i // 2, i % 2
    rows, feats = tokens.shape
    cap = rows * routes.shape[1] * 3 // (2 * groups)

    def over_y(a):
        return lax.ppermute(a, "group", [(j, j ^ 1) for j in range(groups)])

    def over_z(a):
        return lax.ppermute(a, "group", [(j, (j + 2) % groups) for j in range(groups)])

    def over_core(a):
        return lax.ppermute(a, "inner", [(j, j ^ 1) for j in range(inners)])

    def over_x(a, s):
        return lax.ppermute(a, "inner", [(j, (j + 2 * s) % inners) for j in range(inners)])

    came = [(x - s) % chips * 2 for s in range(chips)]
    goes = [(x + s) % chips * 2 for s in range(chips)]
    order = jnp.stack(
        [k + c for k in came] + [k + 1 - c for k in came] + [k + 1 - c for k in goes] + [k + c for k in goes]
    ).astype(jnp.int32)

    at = jnp.full((1,), g, jnp.int32)
    block, token = label(tokens, routes, gate_weights, [])
    main, other = [block] + [over_z(block)] * (planes > 1), [over_y(block)]
    choices = routes.shape[1]

    labels, pieces, near, kept, given, own, passed, back, total = {}, {}, {}, {}, {}, {}, {}, {}, None
    stay = {}
    for step, t in schedule(planes):
        if step == "pack":
            after = [token] + ([given[t - 3]] if t - 3 in given else [])
            blocks, before = (main[t], other[t]), pieces.get(t - 1, [])
            p, labels[t], ahead, whole, token = pack(at, blocks, main[t + 1:], before, rows, choices, cap, after)
            other += [over_y(a) for a in ahead]
            main += [over_z(a) for a in ahead if t + 2 < planes]
            pieces[t] = [p] + [over_x(p, s) for s in range(1, chips)]
            near.update((t - 1, (a, over_core(a))) for a in whole)
        elif step == "join":
            a, token = join(pieces[t], [token])
            near[t] = a, over_core(a)
        elif step == "expert":
            give, kept[t], token = expert(order, *near[t], feats, w_gate, w_up, w_down, [token])
            given[t] = over_core(give)
        elif step == "pair":
            (own[t], *sums), token = pair_sum(kept[t], given[t], feats, [token])
            passed[t] = [over_x(a, s + 1) for s, a in enumerate(sums)]
        else:
            stay[t], go, token = spread(at, labels[t], choices, [own[t], *passed[t]], [token])
            back[t] = over_y(go)
            value = stay[t] + back[t].astype(F32)
            total = (value if total is None else value + over_z(total).astype(F32)).astype(BF)
    return total


def schedule(planes):
    last = planes - 1
    steps = [("pack", 0)]
    for t in range(1, planes):
        steps += [("pack", t), ("expert", t - 1)]
    steps += [("join", last), ("expert", last)]
    steps += [("pair", t) for t in range(last - 1, 0, -1)]
    for t in range(1, planes):
        if t == max(last - 1, 1):
            steps += [("pair", last)]
        steps += [("spread", t)]
    return steps + [("pair", 0), ("spread", 0)]


def solution(mesh):
    placed = (
        P("group", "inner"),
        P("group", None),
        P("group", None),
        P("group", None, "inner"),
        P("group", None, "inner"),
        P("group", "inner", None),
    )
    return jax.shard_map(
        local, mesh=mesh, in_specs=placed, out_specs=P("group", "inner"), check_vma=False
    )
```

time: 368 us -> 191 us (0.52)
  local copies, waits for them, and re-layouts: 124 us -> 21.8 us
  matrix products: 70.8 us -> 0 us
  Pallas kernels: 0 us -> 40 us
  other arithmetic: 23.1 us -> 1.29 us
  starting transfers between devices: 42.5 us -> 30.1 us
  waiting for transfers between devices: 104 us -> 97.3 us
    dot_general x25 -> x0, matrix products: 70.8 us -> none  [the longest x4 41.9 us: local(): part = jnp.dot(hidden, w_down[0], preferred_element_type=F32).astype(BF)]
    reshape x8 -> x0, local copies, waits for them, and re-layouts: 69.3 us -> none  [the longest x4 39.5 us: local(): full = jnp.stack([even, odd], axis=2).reshape(2 * cap, depth)]
    pallas_call x0 -> x18, Pallas kernels: none -> 40 us  [the longest x4 32 us: expert(): pl.pallas_call(behind(functools.partial(expert_kernel, half), 6, len(afte...]
    slice x8 -> x0, local copies, waits for them, and re-layouts: 30.7 us -> none  [the longest x4 29.8 us: local(): keep = jnp.where(c == 0, part[:, :, 0], part[:, :, 1])]
    ppermute x16 -> x8, waiting for transfers between devices: 61.6 us -> 36.3 us  [over_x(): lax.ppermute(a, 'inner', [(j, (j + 2 * s) % inners) for j in range(inners)])]
    another operation x4 -> x1, local copies, waits for them, and re-layouts: 17.5 us -> 0.08 us  [local(): jnp.stack([k + c for k in came] + [k + 1 - c for k in came] + [k + 1 - c...]
    unnamed x40 -> x24, local copies, waits for them, and re-layouts: 6.12 us -> 21.7 us
    ppermute x9 -> x6, waiting for transfers between devices: 19.2 us -> 32.5 us  [over_z(): lax.ppermute(a, 'group', [(j, (j + 2) % groups) for j in range(groups)])]
  transfers between devices with their start and end apart: 42 -> 30, of which waited for: 20 -> 18; matrix products, arithmetic and copies ran while one was open for 58% -> 0% of each run, Pallas kernels for 0% -> 19%
where the time goes in v3:
time: 191 us
  waiting for transfers between devices  97.3 us (51%)
  Pallas kernels  40 us (21%)
  starting transfers between devices  30.1 us (16%)
  local copies, waits for them, and re-layouts  21.8 us (11%)
    ppermute x8, waiting for transfers between devices, over_x(): lax.ppermute(a, 'inner', [(j, (j + 2 * s) % inners) for j in range(inners)])  36.3 us
    ppermute x6, waiting for transfers between devices, over_z(): lax.ppermute(a, 'group', [(j, (j + 2) % groups) for j in range(groups)])  32.5 us
    pallas_call x4, Pallas kernels, expert(): pl.pallas_call(behind(functools.partial(expert_kernel, half), 6, len(afte...  32 us
    ppermute x8, waiting for transfers between devices, over_y(): return lax.ppermute(a, 'group', [(j, j ^ 1) for j in range(groups)])  23.3 us
    unnamed x24, local copies, waits for them, and re-layouts  21.7 us
    ppermute x8, starting transfers between devices, over_x(): lax.ppermute(a, 'inner', [(j, (j + 2 * s) % inners) for j in range(inners)])  10.3 us
    ppermute x8, starting transfers between devices, over_y(): return lax.ppermute(a, 'group', [(j, j ^ 1) for j in range(groups)])  9.67 us
    ppermute x6, starting transfers between devices, over_z(): lax.ppermute(a, 'group', [(j, (j + 2) % groups) for j in range(groups)])  9.15 us
  transfers between devices with their start and end apart: 30, of which 18 were waited for; matrix products, arithmetic and copies ran while one was open for 0% of the time, Pallas kernels for 19%

profile of v3, /device:TPU:0, one launch (start us, length us, event | category | flops | bytes accessed | tf_op | source)
XLA Modules:
  0.0 190.7 jit_solution(14314071773328883724)
XLA Ops:
  2.4 3.1 %collective-permute-start.1 = (bf16[144,1792]{1,0:T(8,128)(2,1)S(1)}, bf16[144,1792]{1,0:T(8,128)(2,1)S(1)}, u32[]{:S(2)}, u32[]{:S(2)}) collective-permute-start(bf16[144,1792]{1,0:T(8,128)(2,1)S(1)} %get-tuple-element.62.refs_1_), channel_id=1, source_target_pairs={{0,8},{4,12},{8,16},{12,20},{16,24},{20,28},{24,0},{28,4},{1,9},{5... | collective-permute-start | bytes 1548296 | tf_op jit(solution)/shard_map/ppermute | solution.py:237
  7.0 12.3 %collective-permute-done.1.refs_3_.refs_1_ = bf16[144,1792]{1,0:T(8,128)(2,1)S(1)} collective-permute-done((bf16[144,1792]{1,0:T(8,128)(2,1)S(1)}, bf16[144,1792]{1,0:T(8,128)(2,1)S(1)}, u32[]{:S(2)}, u32[]{:S(2)}) %collective-permute-start.1) | collective-permute-done | bytes 516128 | tf_op jit(solution)/shard_map/ppermute | solution.py:237
  24.0 11.7 %collective-permute-done.3.refs_3_.refs_1_ = bf16[144,1792]{1,0:T(8,128)(2,1)S(1)} collective-permute-done((bf16[144,1792]{1,0:T(8,128)(2,1)S(1)}, bf16[144,1792]{1,0:T(8,128)(2,1)S(1)}, u32[]{:S(2)}, u32[]{:S(2)}) %collective-permute-start.3) | collective-permute-done | bytes 516128 | tf_op jit(solution)/shard_map/ppermute | solution.py:237
  41.6 3.1 %copy-done = bf16[1,7168,512]{2,1,0:T(8,128)(2,1)S(1)} copy-done((bf16[1,7168,512]{2,1,0:T(8,128)(2,1)S(1)}, bf16[1,7168,512]{2,1,0:T(8,128)(2,1)}, u32[]{:S(2)}) %copy-start) | copy-done | bytes 7340056
  44.7 3.1 %copy-done.2 = bf16[1,7168,512]{2,1,0:T(8,128)(2,1)S(1)} copy-done((bf16[1,7168,512]{2,1,0:T(8,128)(2,1)S(1)}, bf16[1,7168,512]{2,1,0:T(8,128)(2,1)}, u32[]{:S(2)}) %copy-start.2) | copy-done | bytes 7340056
  47.8 3.1 %copy-done.4 = bf16[1,512,7168]{2,1,0:T(8,128)(2,1)S(1)} copy-done((bf16[1,512,7168]{2,1,0:T(8,128)(2,1)S(1)}, bf16[1,512,7168]{2,1,0:T(8,128)(2,1)}, u32[]{:S(2)}) %copy-start.4) | copy-done | bytes 7340056
  50.8 8.0 %shard_map.67 = (bf16[192,3584]{1,0:T(8,128)(2,1)S(1)}, bf16[192,3584]{1,0:T(8,128)(2,1)S(1)}, f32[8,128]{1,0:T(8,128)S(1)}) custom-call(s32[8]{0:T(128)S(1)} %stack.29.refs_0_, bf16[192,3584]{1,0:T(8,128)(2,1)S(1)} %get-tuple-element.68.refs_1_, bf16[192,3584]{1,0:T(8,128)(2,1)S(1)} %collective-permute-done.5.refs_2_, bf16[1,7168,512]{2,1,0:T(8,128)(2,1)S(1)} %copy-done, ...), custom_call_target="tpu_custom_call" | custom-call | flops 40000000000 | bytes 1024 | tf_op jit(solution)/shard_map/pallas_call | solution.py:216
  62.8 3.1 %copy-done.1 = bf16[1,7168,512]{2,1,0:T(8,128)(2,1)S(1)} copy-done((bf16[1,7168,512]{2,1,0:T(8,128)(2,1)S(1)}, bf16[1,7168,512]{2,1,0:T(8,128)(2,1)}, u32[]{:S(2)}) %copy-start.1) | copy-done | bytes 7340056
  65.9 3.1 %copy-done.3 = bf16[1,7168,512]{2,1,0:T(8,128)(2,1)S(1)} copy-done((bf16[1,7168,512]{2,1,0:T(8,128)(2,1)S(1)}, bf16[1,7168,512]{2,1,0:T(8,128)(2,1)}, u32[]{:S(2)}) %copy-start.3) | copy-done | bytes 7340056
  68.9 3.1 %copy-done.5 = bf16[1,512,7168]{2,1,0:T(8,128)(2,1)S(1)} copy-done((bf16[1,512,7168]{2,1,0:T(8,128)(2,1)S(1)}, bf16[1,512,7168]{2,1,0:T(8,128)(2,1)}, u32[]{:S(2)}) %copy-start.5) | copy-done | bytes 7340056
  72.0 8.0 %shard_map.69 = (bf16[192,3584]{1,0:T(8,128)(2,1)S(1)}, bf16[192,3584]{1,0:T(8,128)(2,1)S(1)}, f32[8,128]{1,0:T(8,128)S(1)}) custom-call(s32[8]{0:T(128)S(1)} %stack.29.refs_0_, bf16[192,3584]{1,0:T(8,128)(2,1)S(1)} %get-tuple-element.77.refs_1_, bf16[192,3584]{1,0:T(8,128)(2,1)S(1)} %collective-permute-done.12.refs_2_, bf16[1,7168,512]{2,1,0:T(8,128)(2,1)S(1)} %copy-done.1, ...), custom_call_target="tpu_custom_call" | custom-call | flops 40000000000 | bytes 1024 | tf_op jit(solution)/shard_map/pallas_call | solution.py:216
  83.9 8.0 %shard_map.71 = (bf16[192,3584]{1,0:T(8,128)(2,1)S(1)}, bf16[192,3584]{1,0:T(8,128)(2,1)S(1)}, f32[8,128]{1,0:T(8,128)S(1)}) custom-call(s32[8]{0:T(128)S(1)} %stack.29.refs_0_, bf16[192,3584]{1,0:T(8,128)(2,1)S(1)} %get-tuple-element.82.refs_1_, bf16[192,3584]{1,0:T(8,128)(2,1)S(1)} %collective-permute-done.14.refs_2_, bf16[1,7168,512]{2,1,0:T(8,128)(2,1)S(1)} %copy-done.1, ...), custom_call_target="tpu_custom_call" | custom-call | flops 40000000000 | bytes 1024 | tf_op jit(solution)/shard_map/pallas_call | solution.py:216
  91.9 6.8 %collective-permute-done.13.refs_1_ = bf16[192,1792]{1,0:T(8,128)(2,1)S(1)} collective-permute-done((bf16[192,1792]{1,0:T(8,128)(2,1)S(1)}, bf16[192,1792]{1,0:T(8,128)(2,1)S(1)}, u32[]{:S(2)}, u32[]{:S(2)}) %collective-permute-start.13) | collective-permute-done | bytes 688160 | tf_op jit(solution)/shard_map/ppermute | solution.py:243
  99.4 2.5 %collective-permute-done.15.refs_2_ = bf16[192,3584]{1,0:T(8,128)(2,1)S(1)} collective-permute-done((bf16[192,3584]{1,0:T(8,128)(2,1)S(1)}, bf16[192,3584]{1,0:T(8,128)(2,1)S(1)}, u32[]{:S(2)}, u32[]{:S(2)}) %collective-permute-start.15) | collective-permute-done | bytes 1376288 | tf_op jit(solution)/shard_map/ppermute | solution.py:240
  101.9 8.1 %shard_map.73 = (bf16[192,3584]{1,0:T(8,128)(2,1)S(1)}, bf16[192,3584]{1,0:T(8,128)(2,1)S(1)}, f32[8,128]{1,0:T(8,128)S(1)}) custom-call(s32[8]{0:T(128)S(1)} %stack.29.refs_0_, bf16[192,3584]{1,0:T(8,128)(2,1)S(1)} %get-tuple-element.85.refs_1_, bf16[192,3584]{1,0:T(8,128)(2,1)S(1)} %collective-permute-done.15.refs_2_, bf16[1,7168,512]{2,1,0:T(8,128)(2,1)S(1)} %copy-done.1, ...), custom_call_target="tpu_custom_call" | custom-call | flops 40000000000 | bytes 1024 | tf_op jit(solution)/shard_map/pallas_call | solution.py:216
  111.6 16.6 %collective-permute-done.19.refs_3_ = bf16[192,1792]{1,0:T(8,128)(2,1)S(1)} collective-permute-done((bf16[192,1792]{1,0:T(8,128)(2,1)S(1)}, bf16[192,1792]{1,0:T(8,128)(2,1)S(1)}, u32[]{:S(2)}, u32[]{:S(2)}) %collective-permute-start.19) | collective-permute-done | bytes 688160 | tf_op jit(solution)/shard_map/ppermute | solution.py:243
  131.7 9.3 %collective-permute-done.26 = bf16[128,1792]{1,0:T(8,128)(2,1)S(1)} collective-permute-done((bf16[128,1792]{1,0:T(8,128)(2,1)S(1)}, bf16[128,1792]{1,0:T(8,128)(2,1)S(1)}, u32[]{:S(2)}, u32[]{:S(2)}) %collective-permute-start.26) | collective-permute-done | bytes 458784 | tf_op jit(solution)/shard_map/ppermute | solution.py:234
  143.0 3.6 %collective-permute-done.21.refs_3_ = bf16[192,1792]{1,0:T(8,128)(2,1)S(1)} collective-permute-done((bf16[192,1792]{1,0:T(8,128)(2,1)S(1)}, bf16[192,1792]{1,0:T(8,128)(2,1)S(1)}, u32[]{:S(2)}, u32[]{:S(2)}) %collective-permute-start.21) | collective-permute-done | bytes 688160 | tf_op jit(solution)/shard_map/ppermute | solution.py:243
  149.6 4.1 %collective-permute-done.27 = bf16[128,1792]{1,0:T(8,128)(2,1)S(1)} collective-permute-done((bf16[128,1792]{1,0:T(8,128)(2,1)S(1)}, bf16[128,1792]{1,0:T(8,128)(2,1)S(1)}, u32[]{:S(2)}, u32[]{:S(2)}) %collective-permute-start.27) | collective-permute-done | bytes 458784 | tf_op jit(solution)/shard_map/ppermute | solution.py:237
  153.7 4.4 %collective-permute-done.25 = bf16[128,1792]{1,0:T(8,128)(2,1)S(1)} collective-permute-done((bf16[128,1792]{1,0:T(8,128)(2,1)S(1)}, bf16[128,1792]{1,0:T(8,128)(2,1)S(1)}, u32[]{:S(2)}, u32[]{:S(2)}) %collective-permute-start.25) | collective-permute-done | bytes 458784 | tf_op jit(solution)/shard_map/ppermute | solution.py:234
  159.5 4.4 %collective-permute-done.20.refs_3_ = bf16[192,1792]{1,0:T(8,128)(2,1)S(1)} collective-permute-done((bf16[192,1792]{1,0:T(8,128)(2,1)S(1)}, bf16[192,1792]{1,0:T(8,128)(2,1)S(1)}, u32[]{:S(2)}, u32[]{:S(2)}) %collective-permute-start.20) | collective-permute-done | bytes 688160 | tf_op jit(solution)/shard_map/ppermute | solution.py:243
  169.7 4.5 %collective-permute-done.24 = bf16[128,1792]{1,0:T(8,128)(2,1)S(1)} collective-permute-done((bf16[128,1792]{1,0:T(8,128)(2,1)S(1)}, bf16[128,1792]{1,0:T(8,128)(2,1)S(1)}, u32[]{:S(2)}, u32[]{:S(2)}) %collective-permute-start.24) | collective-permute-done | bytes 458784 | tf_op jit(solution)/shard_map/ppermute | solution.py:234
  176.1 4.1 %collective-permute-done.22.refs_3_ = bf16[192,1792]{1,0:T(8,128)(2,1)S(1)} collective-permute-done((bf16[192,1792]{1,0:T(8,128)(2,1)S(1)}, bf16[192,1792]{1,0:T(8,128)(2,1)S(1)}, u32[]{:S(2)}, u32[]{:S(2)}) %collective-permute-start.22) | collective-permute-done | bytes 688160 | tf_op jit(solution)/shard_map/ppermute | solution.py:243
  184.8 5.0 %collective-permute-done.23 = bf16[128,1792]{1,0:T(8,128)(2,1)S(1)} collective-permute-done((bf16[128,1792]{1,0:T(8,128)(2,1)S(1)}, bf16[128,1792]{1,0:T(8,128)(2,1)S(1)}, u32[]{:S(2)}, u32[]{:S(2)}) %collective-permute-start.23) | collective-permute-done | bytes 458784 | tf_op jit(solution)/shard_map/ppermute | solution.py:234
  (83 shorter events, 47.6 us)
Async XLA Ops:
  2.4 16.8 %collective-permute-start.1 = (bf16[144,1792]{1,0:T(8,128)(2,1)S(1)}, bf16[144,1792]{1,0:T(8,128)(2,1)S(1)}, u32[]{:S(2)}, u32[]{:S(2)}) collective-permute-start(bf16[144,1792]{1,0:T(8,128)(2,1)S(1)} %get-tuple-element.62.refs_1_), channel_id=1, source_target_pairs={{0,8},{4,12},{8,16},{12,20},{16,24},{20,28},{24,0},{28,4},{1,9},{5... | collective-permute-start | bytes 1548296 | tf_op jit(solution)/shard_map/ppermute | solution.py:237
  5.5 13.8 %collective-permute-start = (bf16[144,1792]{1,0:T(8,128)(2,1)S(1)}, bf16[144,1792]{1,0:T(8,128)(2,1)S(1)}, u32[]{:S(2)}, u32[]{:S(2)}) collective-permute-start(bf16[144,1792]{1,0:T(8,128)(2,1)S(1)} %get-tuple-element.62.refs_1_), channel_id=1, source_target_pairs={{0,4},{4,0},{8,12},{12,8},{16,20},{20,16},{24,28},{28,24},{1,5},{5... | collective-permute-start | bytes 1548296 | tf_op jit(solution)/shard_map/ppermute | solution.py:234
  19.9 16.7 %collective-permute-start.4 = (bf16[192,1792]{1,0:T(8,128)(2,1)S(1)}, bf16[192,1792]{1,0:T(8,128)(2,1)S(1)}, u32[]{:S(2)}, u32[]{:S(2)}) collective-permute-start(bf16[192,1792]{1,0:T(8,128)(2,1)S(1)} %get-tuple-element.66.refs_4_), channel_id=1, source_target_pairs={{0,2},{1,3},{2,0},{3,1},{4,6},{5,7},{6,4},{7,5},{8,10},{9,11},{10,... | collective-permute-start | bytes 2064392 | tf_op jit(solution)/shard_map/ppermute | solution.py:243
  21.5 14.2 %collective-permute-start.3 = (bf16[144,1792]{1,0:T(8,128)(2,1)S(1)}, bf16[144,1792]{1,0:T(8,128)(2,1)S(1)}, u32[]{:S(2)}, u32[]{:S(2)}) collective-permute-start(bf16[144,1792]{1,0:T(8,128)(2,1)S(1)} %get-tuple-element.65), channel_id=1, source_target_pairs={{0,8},{4,12},{8,16},{12,20},{16,24},{20,28},{24,0},{28,4},{1,9},{5... | collective-permute-start | bytes 1548296 | tf_op jit(solution)/shard_map/ppermute | solution.py:237
  22.5 13.2 %collective-permute-start.2 = (bf16[144,1792]{1,0:T(8,128)(2,1)S(1)}, bf16[144,1792]{1,0:T(8,128)(2,1)S(1)}, u32[]{:S(2)}, u32[]{:S(2)}) collective-permute-start(bf16[144,1792]{1,0:T(8,128)(2,1)S(1)} %get-tuple-element.65), channel_id=1, source_target_pairs={{0,4},{4,0},{8,12},{12,8},{16,20},{20,16},{24,28},{28,24},{1,5},{5... | collective-permute-start | bytes 1548296 | tf_op jit(solution)/shard_map/ppermute | solution.py:234
  38.2 20.6 %collective-permute-start.8 = (bf16[144,1792]{1,0:T(8,128)(2,1)}, bf16[144,1792]{1,0:T(8,128)(2,1)S(1)}, u32[]{:S(2)}, u32[]{:S(2)}) collective-permute-start(bf16[144,1792]{1,0:T(8,128)(2,1)} %copy-done.8), channel_id=1, source_target_pairs={{0,4},{4,0},{8,12},{12,8},{16,20},{20,16},{24,28},{28,24},{1,5},{5... | collective-permute-start | bytes 1548296 | tf_op jit(solution)/shard_map/ppermute | solution.py:234
  39.5 19.4 %collective-permute-start.7 = (bf16[144,1792]{1,0:T(8,128)(2,1)}, bf16[144,1792]{1,0:T(8,128)(2,1)S(1)}, u32[]{:S(2)}, u32[]{:S(2)}) collective-permute-start(bf16[144,1792]{1,0:T(8,128)(2,1)} %copy-done.8), channel_id=1, source_target_pairs={{0,8},{4,12},{8,16},{12,20},{16,24},{20,28},{24,0},{28,4},{1,9},{5... | collective-permute-start | bytes 1548296 | tf_op jit(solution)/shard_map/ppermute | solution.py:237
  40.1 18.7 %collective-permute-start.9 = (bf16[192,1792]{1,0:T(8,128)(2,1)S(1)}, bf16[192,1792]{1,0:T(8,128)(2,1)S(1)}, u32[]{:S(2)}, u32[]{:S(2)}) collective-permute-start(bf16[192,1792]{1,0:T(8,128)(2,1)S(1)} %get-tuple-element.73.refs_4_), channel_id=1, source_target_pairs={{0,2},{1,3},{2,0},{3,1},{4,6},{5,7},{6,4},{7,5},{8,10},{9,11},{10,... | collective-permute-start | bytes 2064392 | tf_op jit(solution)/shard_map/ppermute | solution.py:243
  59.6 20.3 %collective-permute-start.10 = (bf16[144,1792]{1,0:T(8,128)(2,1)S(1)}, bf16[144,1792]{1,0:T(8,128)(2,1)S(1)}, u32[]{:S(2)}, u32[]{:S(2)}) collective-permute-start(bf16[144,1792]{1,0:T(8,128)(2,1)S(1)} %get-tuple-element.75), channel_id=1, source_target_pairs={{0,4},{4,0},{8,12},{12,8},{16,20},{20,16},{24,28},{28,24},{1,5},{5... | collective-permute-start | bytes 1548296 | tf_op jit(solution)/shard_map/ppermute | solution.py:234
  60.7 19.3 %collective-permute-start.11 = (bf16[192,1792]{1,0:T(8,128)(2,1)S(1)}, bf16[192,1792]{1,0:T(8,128)(2,1)S(1)}, u32[]{:S(2)}, u32[]{:S(2)}) collective-permute-start(bf16[192,1792]{1,0:T(8,128)(2,1)S(1)} %get-tuple-element.76.refs_3_), channel_id=1, source_target_pairs={{0,2},{1,3},{2,0},{3,1},{4,6},{5,7},{6,4},{7,5},{8,10},{9,11},{10,... | collective-permute-start | bytes 2064392 | tf_op jit(solution)/shard_map/ppermute | solution.py:243
  62.2 17.8 %collective-permute-start.6 = (bf16[192,3584]{1,0:T(8,128)(2,1)S(1)}, bf16[192,3584]{1,0:T(8,128)(2,1)S(1)}, u32[]{:S(2)}, u32[]{:S(2)}) collective-permute-start(bf16[192,3584]{1,0:T(8,128)(2,1)S(1)} %get-tuple-element.71), channel_id=1, source_target_pairs={{0,1},{1,0},{2,3},{3,2},{4,5},{5,4},{6,7},{7,6},{8,9},{9,8},{10,11... | collective-permute-start | bytes 4128776 | tf_op jit(solution)/shard_map/ppermute | solution.py:240
  80.9 17.7 %collective-permute-start.13 = (bf16[192,1792]{1,0:T(8,128)(2,1)S(1)}, bf16[192,1792]{1,0:T(8,128)(2,1)S(1)}, u32[]{:S(2)}, u32[]{:S(2)}) collective-permute-start(bf16[192,1792]{1,0:T(8,128)(2,1)S(1)} %get-tuple-element.81.refs_0_), channel_id=1, source_target_pairs={{0,2},{1,3},{2,0},{3,1},{4,6},{5,7},{6,4},{7,5},{8,10},{9,11},{10,... | collective-permute-start | bytes 2064392 | tf_op jit(solution)/shard_map/ppermute | solution.py:243
  98.8 11.6 %collective-permute-start.17 = (bf16[192,3584]{1,0:T(8,128)(2,1)S(1)}, bf16[192,3584]{1,0:T(8,128)(2,1)S(1)}, u32[]{:S(2)}, u32[]{:S(2)}) collective-permute-start(bf16[192,3584]{1,0:T(8,128)(2,1)S(1)} %get-tuple-element.91), channel_id=1, source_target_pairs={{0,1},{1,0},{2,3},{3,2},{4,5},{5,4},{6,7},{7,6},{8,9},{9,8},{10,11... | collective-permute-start | bytes 4128776 | tf_op jit(solution)/shard_map/ppermute | solution.py:240
  99.3 10.8 %collective-permute-start.18 = (bf16[192,3584]{1,0:T(8,128)(2,1)S(1)}, bf16[192,3584]{1,0:T(8,128)(2,1)S(1)}, u32[]{:S(2)}, u32[]{:S(2)}) collective-permute-start(bf16[192,3584]{1,0:T(8,128)(2,1)S(1)} %get-tuple-element.93), channel_id=1, source_target_pairs={{0,1},{1,0},{2,3},{3,2},{4,5},{5,4},{6,7},{7,6},{8,9},{9,8},{10,11... | collective-permute-start | bytes 4128776 | tf_op jit(solution)/shard_map/ppermute | solution.py:240
  110.7 17.5 %collective-permute-start.19 = (bf16[192,1792]{1,0:T(8,128)(2,1)S(1)}, bf16[192,1792]{1,0:T(8,128)(2,1)S(1)}, u32[]{:S(2)}, u32[]{:S(2)}) collective-permute-start(bf16[192,1792]{1,0:T(8,128)(2,1)S(1)} %get-tuple-element.97), channel_id=1, source_target_pairs={{0,2},{1,3},{2,0},{3,1},{4,6},{5,7},{6,4},{7,5},{8,10},{9,11},{10,... | collective-permute-start | bytes 2064392 | tf_op jit(solution)/shard_map/ppermute | solution.py:243
  111.6 31.1 %collective-permute-start.16 = (bf16[192,3584]{1,0:T(8,128)(2,1)S(1)}, bf16[192,3584]{1,0:T(8,128)(2,1)S(1)}, u32[]{:S(2)}, u32[]{:S(2)}) collective-permute-start(bf16[192,3584]{1,0:T(8,128)(2,1)S(1)} %get-tuple-element.88), channel_id=1, source_target_pairs={{0,1},{1,0},{2,3},{3,2},{4,5},{5,4},{6,7},{7,6},{8,9},{9,8},{10,11... | collective-permute-start | bytes 4128776 | tf_op jit(solution)/shard_map/ppermute | solution.py:240
  129.2 11.8 %collective-permute-start.26 = (bf16[128,1792]{1,0:T(8,128)(2,1)S(1)}, bf16[128,1792]{1,0:T(8,128)(2,1)S(1)}, u32[]{:S(2)}, u32[]{:S(2)}) collective-permute-start(bf16[128,1792]{1,0:T(8,128)(2,1)S(1)} %get-tuple-element.118), channel_id=1, source_target_pairs={{0,4},{4,0},{8,12},{12,8},{16,20},{20,16},{24,28},{28,24},{1,5},{5... | collective-permute-start | bytes 1376264 | tf_op jit(solution)/shard_map/ppermute | solution.py:234
  130.2 16.4 %collective-permute-start.21 = (bf16[192,1792]{1,0:T(8,128)(2,1)S(1)}, bf16[192,1792]{1,0:T(8,128)(2,1)S(1)}, u32[]{:S(2)}, u32[]{:S(2)}) collective-permute-start(bf16[192,1792]{1,0:T(8,128)(2,1)S(1)} %get-tuple-element.104), channel_id=1, source_target_pairs={{0,2},{1,3},{2,0},{3,1},{4,6},{5,7},{6,4},{7,5},{8,10},{9,11},{10,... | collective-permute-start | bytes 2064392 | tf_op jit(solution)/shard_map/ppermute | solution.py:243
  141.1 12.7 %collective-permute-start.27 = (bf16[128,1792]{1,0:T(8,128)(2,1)S(1)}, bf16[128,1792]{1,0:T(8,128)(2,1)S(1)}, u32[]{:S(2)}, u32[]{:S(2)}) collective-permute-start(bf16[128,1792]{1,0:T(8,128)(2,1)S(1)} %add_convert_fusion.3), channel_id=1, source_target_pairs={{0,8},{4,12},{8,16},{12,20},{16,24},{20,28},{24,0},{28,4},{1,9},{5... | collective-permute-start | bytes 1376264 | tf_op jit(solution)/shard_map/ppermute | solution.py:237
  147.6 10.6 %collective-permute-start.25 = (bf16[128,1792]{1,0:T(8,128)(2,1)S(1)}, bf16[128,1792]{1,0:T(8,128)(2,1)S(1)}, u32[]{:S(2)}, u32[]{:S(2)}) collective-permute-start(bf16[128,1792]{1,0:T(8,128)(2,1)S(1)} %get-tuple-element.116), channel_id=1, source_target_pairs={{0,4},{4,0},{8,12},{12,8},{16,20},{20,16},{24,28},{28,24},{1,5},{5... | collective-permute-start | bytes 1376264 | tf_op jit(solution)/shard_map/ppermute | solution.py:234
  148.7 15.2 %collective-permute-start.20 = (bf16[192,1792]{1,0:T(8,128)(2,1)S(1)}, bf16[192,1792]{1,0:T(8,128)(2,1)S(1)}, u32[]{:S(2)}, u32[]{:S(2)}) collective-permute-start(bf16[192,1792]{1,0:T(8,128)(2,1)S(1)} %get-tuple-element.101), channel_id=1, source_target_pairs={{0,2},{1,3},{2,0},{3,1},{4,6},{5,7},{6,4},{7,5},{8,10},{9,11},{10,... | collective-permute-start | bytes 2064392 | tf_op jit(solution)/shard_map/ppermute | solution.py:243
  158.3 11.4 %collective-permute-start.28 = (bf16[128,1792]{1,0:T(8,128)(2,1)S(1)}, bf16[128,1792]{1,0:T(8,128)(2,1)S(1)}, u32[]{:S(2)}, u32[]{:S(2)}) collective-permute-start(bf16[128,1792]{1,0:T(8,128)(2,1)S(1)} %add_convert_fusion.2), channel_id=1, source_target_pairs={{0,8},{4,12},{8,16},{12,20},{16,24},{20,28},{24,0},{28,4},{1,9},{5... | collective-permute-start | bytes 1376264 | tf_op jit(solution)/shard_map/ppermute | solution.py:237
  166.2 14.0 %collective-permute-start.22 = (bf16[192,1792]{1,0:T(8,128)(2,1)S(1)}, bf16[192,1792]{1,0:T(8,128)(2,1)S(1)}, u32[]{:S(2)}, u32[]{:S(2)}) collective-permute-start(bf16[192,1792]{1,0:T(8,128)(2,1)S(1)} %get-tuple-element.109), channel_id=1, source_target_pairs={{0,2},{1,3},{2,0},{3,1},{4,6},{5,7},{6,4},{7,5},{8,10},{9,11},{10,... | collective-permute-start | bytes 2064392 | tf_op jit(solution)/shard_map/ppermute | solution.py:243
  174.4 10.3 %collective-permute-start.29 = (bf16[128,1792]{1,0:T(8,128)(2,1)S(1)}, bf16[128,1792]{1,0:T(8,128)(2,1)S(1)}, u32[]{:S(2)}, u32[]{:S(2)}) collective-permute-start(bf16[128,1792]{1,0:T(8,128)(2,1)S(1)} %add_convert_fusion.1), channel_id=1, source_target_pairs={{0,8},{4,12},{8,16},{12,20},{16,24},{20,28},{24,0},{28,4},{1,9},{5... | collective-permute-start | bytes 1376264 | tf_op jit(solution)/shard_map/ppermute | solution.py:237
  (18 other events, 62.3 us)

commit v4 on v3

--- a/solution.py
+++ b/solution.py
@@ -10,7 +10,7 @@
 BF = jnp.bfloat16
 F32 = jnp.float32
 TOKEN = jax.ShapeDtypeStruct((8, 128), F32)
-PACK, EXPERT, PAIR, SPREAD, LABEL = 10, 40, 0.7, 1.5, 1.0
+PACK, EXPERT, PAIR, SPREAD, LABEL = 10, 40, 2, 20, 1
 VMEM_MIB, EXPERT_MIB = 12, 22
 
 
@@ -285,13 +285,10 @@
     last = planes - 1
     steps = [("pack", 0)]
     for t in range(1, planes):
-        steps += [("pack", t), ("expert", t - 1)]
-    steps += [("join", last), ("expert", last)]
-    steps += [("pair", t) for t in range(last - 1, 0, -1)]
+        steps += [("pack", t), ("expert", t - 1)] + [("pair", t - 2)] * (t > 2)
+    steps += [("join", last)] + [("pair", last - 1)] * (last > 1) + [("expert", last)]
     for t in range(1, planes):
-        if t == max(last - 1, 1):
-            steps += [("pair", last)]
-        steps += [("spread", t)]
+        steps += [("pair", last)] * (t == min(2, last)) + [("spread", t)]
     return steps + [("pair", 0), ("spread", 0)]
 
 

time: 191 us -> 181 us (0.948)
  waiting for transfers between devices: 97.3 us -> 86.6 us
    ppermute x8, waiting for transfers between devices: 36.3 us -> 25.7 us  [over_x(): lax.ppermute(a, 'inner', [(j, (j + 2 * s) % inners) for j in range(inners)])]
  transfers between devices with their start and end apart: 30 -> 30, of which waited for: 18 -> 18; matrix products, arithmetic and copies ran while one was open for 0% -> 0% of each run, Pallas kernels for 19% -> 21%
where the time goes in v4:
time: 181 us; the launch traced here: 180 us
  waiting for transfers between devices  86.6 us (48%)
  Pallas kernels  40 us (22%)
  starting transfers between devices  30.3 us (17%)
  local copies, waits for them, and re-layouts  21.8 us (12%)
    ppermute x6, waiting for transfers between devices, over_z(): lax.ppermute(a, 'group', [(j, (j + 2) % groups) for j in range(groups)])  33.5 us
    pallas_call x4, Pallas kernels, expert(): pl.pallas_call(behind(functools.partial(expert_kernel, half), 6, len(afte...  32 us
    ppermute x8, waiting for transfers between devices, over_x(): lax.ppermute(a, 'inner', [(j, (j + 2 * s) % inners) for j in range(inners)])  25.7 us
    ppermute x8, waiting for transfers between devices, over_y(): return lax.ppermute(a, 'group', [(j, j ^ 1) for j in range(groups)])  23.3 us
    unnamed x24, local copies, waits for them, and re-layouts  21.7 us
    ppermute x8, starting transfers between devices, over_x(): lax.ppermute(a, 'inner', [(j, (j + 2 * s) % inners) for j in range(inners)])  10.3 us
    ppermute x8, starting transfers between devices, over_y(): return lax.ppermute(a, 'group', [(j, j ^ 1) for j in range(groups)])  9.69 us
    ppermute x6, starting transfers between devices, over_z(): lax.ppermute(a, 'group', [(j, (j + 2) % groups) for j in range(groups)])  9.15 us
  transfers between devices with their start and end apart: 30, of which 18 were waited for; matrix products, arithmetic and copies ran while one was open for 0% of the time, Pallas kernels for 21%

profile of v4, /device:TPU:0, one launch (start us, length us, event | category | flops | bytes accessed | tf_op | source)
XLA Modules:
  0.0 180.3 jit_solution(17894613818864774927)
XLA Ops:
  2.4 3.1 %collective-permute-start.1 = (bf16[144,1792]{1,0:T(8,128)(2,1)S(1)}, bf16[144,1792]{1,0:T(8,128)(2,1)S(1)}, u32[]{:S(2)}, u32[]{:S(2)}) collective-permute-start(bf16[144,1792]{1,0:T(8,128)(2,1)S(1)} %get-tuple-element.62.refs_1_), channel_id=1, source_target_pairs={{0,8},{4,12},{8,16},{12,20},{16,24},{20,28},{24,0},{28,4},{1,9},{5... | collective-permute-start | bytes 1548296 | tf_op jit(solution)/shard_map/ppermute | solution.py:237
  7.0 12.3 %collective-permute-done.1.refs_3_.refs_1_ = bf16[144,1792]{1,0:T(8,128)(2,1)S(1)} collective-permute-done((bf16[144,1792]{1,0:T(8,128)(2,1)S(1)}, bf16[144,1792]{1,0:T(8,128)(2,1)S(1)}, u32[]{:S(2)}, u32[]{:S(2)}) %collective-permute-start.1) | collective-permute-done | bytes 516128 | tf_op jit(solution)/shard_map/ppermute | solution.py:237
  24.0 11.7 %collective-permute-done.3.refs_3_.refs_1_ = bf16[144,1792]{1,0:T(8,128)(2,1)S(1)} collective-permute-done((bf16[144,1792]{1,0:T(8,128)(2,1)S(1)}, bf16[144,1792]{1,0:T(8,128)(2,1)S(1)}, u32[]{:S(2)}, u32[]{:S(2)}) %collective-permute-start.3) | collective-permute-done | bytes 516128 | tf_op jit(solution)/shard_map/ppermute | solution.py:237
  41.6 3.1 %copy-done = bf16[1,7168,512]{2,1,0:T(8,128)(2,1)S(1)} copy-done((bf16[1,7168,512]{2,1,0:T(8,128)(2,1)S(1)}, bf16[1,7168,512]{2,1,0:T(8,128)(2,1)}, u32[]{:S(2)}) %copy-start) | copy-done | bytes 7340056
  44.7 3.1 %copy-done.2 = bf16[1,7168,512]{2,1,0:T(8,128)(2,1)S(1)} copy-done((bf16[1,7168,512]{2,1,0:T(8,128)(2,1)S(1)}, bf16[1,7168,512]{2,1,0:T(8,128)(2,1)}, u32[]{:S(2)}) %copy-start.2) | copy-done | bytes 7340056
  47.8 3.1 %copy-done.4 = bf16[1,512,7168]{2,1,0:T(8,128)(2,1)S(1)} copy-done((bf16[1,512,7168]{2,1,0:T(8,128)(2,1)S(1)}, bf16[1,512,7168]{2,1,0:T(8,128)(2,1)}, u32[]{:S(2)}) %copy-start.4) | copy-done | bytes 7340056
  50.8 8.0 %shard_map.67 = (bf16[192,3584]{1,0:T(8,128)(2,1)S(1)}, bf16[192,3584]{1,0:T(8,128)(2,1)S(1)}, f32[8,128]{1,0:T(8,128)S(1)}) custom-call(s32[8]{0:T(128)S(1)} %stack.29.refs_0_, bf16[192,3584]{1,0:T(8,128)(2,1)S(1)} %get-tuple-element.68.refs_1_, bf16[192,3584]{1,0:T(8,128)(2,1)S(1)} %collective-permute-done.5.refs_2_, bf16[1,7168,512]{2,1,0:T(8,128)(2,1)S(1)} %copy-done, ...), custom_call_target="tpu_custom_call" | custom-call | flops 40000000000 | bytes 1024 | tf_op jit(solution)/shard_map/pallas_call | solution.py:216
  62.8 3.1 %copy-done.1 = bf16[1,7168,512]{2,1,0:T(8,128)(2,1)S(1)} copy-done((bf16[1,7168,512]{2,1,0:T(8,128)(2,1)S(1)}, bf16[1,7168,512]{2,1,0:T(8,128)(2,1)}, u32[]{:S(2)}) %copy-start.1) | copy-done | bytes 7340056
  65.9 3.1 %copy-done.3 = bf16[1,7168,512]{2,1,0:T(8,128)(2,1)S(1)} copy-done((bf16[1,7168,512]{2,1,0:T(8,128)(2,1)S(1)}, bf16[1,7168,512]{2,1,0:T(8,128)(2,1)}, u32[]{:S(2)}) %copy-start.3) | copy-done | bytes 7340056
  68.9 3.1 %copy-done.5 = bf16[1,512,7168]{2,1,0:T(8,128)(2,1)S(1)} copy-done((bf16[1,512,7168]{2,1,0:T(8,128)(2,1)S(1)}, bf16[1,512,7168]{2,1,0:T(8,128)(2,1)}, u32[]{:S(2)}) %copy-start.5) | copy-done | bytes 7340056
  72.0 8.0 %shard_map.69 = (bf16[192,3584]{1,0:T(8,128)(2,1)S(1)}, bf16[192,3584]{1,0:T(8,128)(2,1)S(1)}, f32[8,128]{1,0:T(8,128)S(1)}) custom-call(s32[8]{0:T(128)S(1)} %stack.29.refs_0_, bf16[192,3584]{1,0:T(8,128)(2,1)S(1)} %get-tuple-element.77.refs_1_, bf16[192,3584]{1,0:T(8,128)(2,1)S(1)} %collective-permute-done.12.refs_2_, bf16[1,7168,512]{2,1,0:T(8,128)(2,1)S(1)} %copy-done.1, ...), custom_call_target="tpu_custom_call" | custom-call | flops 40000000000 | bytes 1024 | tf_op jit(solution)/shard_map/pallas_call | solution.py:216
  83.9 8.0 %shard_map.71 = (bf16[192,3584]{1,0:T(8,128)(2,1)S(1)}, bf16[192,3584]{1,0:T(8,128)(2,1)S(1)}, f32[8,128]{1,0:T(8,128)S(1)}) custom-call(s32[8]{0:T(128)S(1)} %stack.29.refs_0_, bf16[192,3584]{1,0:T(8,128)(2,1)S(1)} %get-tuple-element.84.refs_1_, bf16[192,3584]{1,0:T(8,128)(2,1)S(1)} %collective-permute-done.15.refs_2_, bf16[1,7168,512]{2,1,0:T(8,128)(2,1)S(1)} %copy-done.1, ...), custom_call_target="tpu_custom_call" | custom-call | flops 40000000000 | bytes 1024 | tf_op jit(solution)/shard_map/pallas_call | solution.py:216
  92.4 6.4 %collective-permute-done.13.refs_1_ = bf16[192,1792]{1,0:T(8,128)(2,1)S(1)} collective-permute-done((bf16[192,1792]{1,0:T(8,128)(2,1)S(1)}, bf16[192,1792]{1,0:T(8,128)(2,1)S(1)}, u32[]{:S(2)}, u32[]{:S(2)}) %collective-permute-start.13) | collective-permute-done | bytes 688160 | tf_op jit(solution)/shard_map/ppermute | solution.py:243
  102.0 8.1 %shard_map.75 = (bf16[192,3584]{1,0:T(8,128)(2,1)S(1)}, bf16[192,3584]{1,0:T(8,128)(2,1)S(1)}, f32[8,128]{1,0:T(8,128)S(1)}) custom-call(s32[8]{0:T(128)S(1)} %stack.29.refs_0_, bf16[192,3584]{1,0:T(8,128)(2,1)S(1)} %get-tuple-element.88.refs_1_, bf16[192,3584]{1,0:T(8,128)(2,1)S(1)} %collective-permute-done.16.refs_2_, bf16[1,7168,512]{2,1,0:T(8,128)(2,1)S(1)} %copy-done.1, ...), custom_call_target="tpu_custom_call" | custom-call | flops 40000000000 | bytes 1024 | tf_op jit(solution)/shard_map/pallas_call | solution.py:216
  110.4 6.4 %collective-permute-done.19.refs_3_ = bf16[192,1792]{1,0:T(8,128)(2,1)S(1)} collective-permute-done((bf16[192,1792]{1,0:T(8,128)(2,1)S(1)}, bf16[192,1792]{1,0:T(8,128)(2,1)S(1)}, u32[]{:S(2)}, u32[]{:S(2)}) %collective-permute-start.19) | collective-permute-done | bytes 688160 | tf_op jit(solution)/shard_map/ppermute | solution.py:243
  120.3 9.7 %collective-permute-done.26 = bf16[128,1792]{1,0:T(8,128)(2,1)S(1)} collective-permute-done((bf16[128,1792]{1,0:T(8,128)(2,1)S(1)}, bf16[128,1792]{1,0:T(8,128)(2,1)S(1)}, u32[]{:S(2)}, u32[]{:S(2)}) %collective-permute-start.26) | collective-permute-done | bytes 458784 | tf_op jit(solution)/shard_map/ppermute | solution.py:234
  132.0 3.5 %collective-permute-done.21.refs_3_ = bf16[192,1792]{1,0:T(8,128)(2,1)S(1)} collective-permute-done((bf16[192,1792]{1,0:T(8,128)(2,1)S(1)}, bf16[192,1792]{1,0:T(8,128)(2,1)S(1)}, u32[]{:S(2)}, u32[]{:S(2)}) %collective-permute-start.21) | collective-permute-done | bytes 688160 | tf_op jit(solution)/shard_map/ppermute | solution.py:243
  138.6 4.5 %collective-permute-done.27 = bf16[128,1792]{1,0:T(8,128)(2,1)S(1)} collective-permute-done((bf16[128,1792]{1,0:T(8,128)(2,1)S(1)}, bf16[128,1792]{1,0:T(8,128)(2,1)S(1)}, u32[]{:S(2)}, u32[]{:S(2)}) %collective-permute-start.27) | collective-permute-done | bytes 458784 | tf_op jit(solution)/shard_map/ppermute | solution.py:237
  143.1 4.4 %collective-permute-done.25 = bf16[128,1792]{1,0:T(8,128)(2,1)S(1)} collective-permute-done((bf16[128,1792]{1,0:T(8,128)(2,1)S(1)}, bf16[128,1792]{1,0:T(8,128)(2,1)S(1)}, u32[]{:S(2)}, u32[]{:S(2)}) %collective-permute-start.25) | collective-permute-done | bytes 458784 | tf_op jit(solution)/shard_map/ppermute | solution.py:234
  148.8 4.4 %collective-permute-done.20.refs_3_ = bf16[192,1792]{1,0:T(8,128)(2,1)S(1)} collective-permute-done((bf16[192,1792]{1,0:T(8,128)(2,1)S(1)}, bf16[192,1792]{1,0:T(8,128)(2,1)S(1)}, u32[]{:S(2)}, u32[]{:S(2)}) %collective-permute-start.20) | collective-permute-done | bytes 688160 | tf_op jit(solution)/shard_map/ppermute | solution.py:243
  159.4 4.5 %collective-permute-done.24 = bf16[128,1792]{1,0:T(8,128)(2,1)S(1)} collective-permute-done((bf16[128,1792]{1,0:T(8,128)(2,1)S(1)}, bf16[128,1792]{1,0:T(8,128)(2,1)S(1)}, u32[]{:S(2)}, u32[]{:S(2)}) %collective-permute-start.24) | collective-permute-done | bytes 458784 | tf_op jit(solution)/shard_map/ppermute | solution.py:234
  165.7 4.1 %collective-permute-done.22.refs_3_ = bf16[192,1792]{1,0:T(8,128)(2,1)S(1)} collective-permute-done((bf16[192,1792]{1,0:T(8,128)(2,1)S(1)}, bf16[192,1792]{1,0:T(8,128)(2,1)S(1)}, u32[]{:S(2)}, u32[]{:S(2)}) %collective-permute-start.22) | collective-permute-done | bytes 688160 | tf_op jit(solution)/shard_map/ppermute | solution.py:243
  172.0 2.7 %collective-permute-done.29 = bf16[128,1792]{1,0:T(8,128)(2,1)S(1)} collective-permute-done((bf16[128,1792]{1,0:T(8,128)(2,1)S(1)}, bf16[128,1792]{1,0:T(8,128)(2,1)S(1)}, u32[]{:S(2)}, u32[]{:S(2)}) %collective-permute-start.29) | collective-permute-done | bytes 458784 | tf_op jit(solution)/shard_map/ppermute | solution.py:237
  174.7 4.7 %collective-permute-done.23 = bf16[128,1792]{1,0:T(8,128)(2,1)S(1)} collective-permute-done((bf16[128,1792]{1,0:T(8,128)(2,1)S(1)}, bf16[128,1792]{1,0:T(8,128)(2,1)S(1)}, u32[]{:S(2)}, u32[]{:S(2)}) %collective-permute-start.23) | collective-permute-done | bytes 458784 | tf_op jit(solution)/shard_map/ppermute | solution.py:234
  (83 shorter events, 47.3 us)
Async XLA Ops:
  2.4 16.8 %collective-permute-start.1 = (bf16[144,1792]{1,0:T(8,128)(2,1)S(1)}, bf16[144,1792]{1,0:T(8,128)(2,1)S(1)}, u32[]{:S(2)}, u32[]{:S(2)}) collective-permute-start(bf16[144,1792]{1,0:T(8,128)(2,1)S(1)} %get-tuple-element.62.refs_1_), channel_id=1, source_target_pairs={{0,8},{4,12},{8,16},{12,20},{16,24},{20,28},{24,0},{28,4},{1,9},{5... | collective-permute-start | bytes 1548296 | tf_op jit(solution)/shard_map/ppermute | solution.py:237
  5.5 13.8 %collective-permute-start = (bf16[144,1792]{1,0:T(8,128)(2,1)S(1)}, bf16[144,1792]{1,0:T(8,128)(2,1)S(1)}, u32[]{:S(2)}, u32[]{:S(2)}) collective-permute-start(bf16[144,1792]{1,0:T(8,128)(2,1)S(1)} %get-tuple-element.62.refs_1_), channel_id=1, source_target_pairs={{0,4},{4,0},{8,12},{12,8},{16,20},{20,16},{24,28},{28,24},{1,5},{5... | collective-permute-start | bytes 1548296 | tf_op jit(solution)/shard_map/ppermute | solution.py:234
  19.9 16.7 %collective-permute-start.4 = (bf16[192,1792]{1,0:T(8,128)(2,1)S(1)}, bf16[192,1792]{1,0:T(8,128)(2,1)S(1)}, u32[]{:S(2)}, u32[]{:S(2)}) collective-permute-start(bf16[192,1792]{1,0:T(8,128)(2,1)S(1)} %get-tuple-element.66.refs_4_), channel_id=1, source_target_pairs={{0,2},{1,3},{2,0},{3,1},{4,6},{5,7},{6,4},{7,5},{8,10},{9,11},{10,... | collective-permute-start | bytes 2064392 | tf_op jit(solution)/shard_map/ppermute | solution.py:243
  21.5 14.2 %collective-permute-start.3 = (bf16[144,1792]{1,0:T(8,128)(2,1)S(1)}, bf16[144,1792]{1,0:T(8,128)(2,1)S(1)}, u32[]{:S(2)}, u32[]{:S(2)}) collective-permute-start(bf16[144,1792]{1,0:T(8,128)(2,1)S(1)} %get-tuple-element.65), channel_id=1, source_target_pairs={{0,8},{4,12},{8,16},{12,20},{16,24},{20,28},{24,0},{28,4},{1,9},{5... | collective-permute-start | bytes 1548296 | tf_op jit(solution)/shard_map/ppermute | solution.py:237
  22.5 13.2 %collective-permute-start.2 = (bf16[144,1792]{1,0:T(8,128)(2,1)S(1)}, bf16[144,1792]{1,0:T(8,128)(2,1)S(1)}, u32[]{:S(2)}, u32[]{:S(2)}) collective-permute-start(bf16[144,1792]{1,0:T(8,128)(2,1)S(1)} %get-tuple-element.65), channel_id=1, source_target_pairs={{0,4},{4,0},{8,12},{12,8},{16,20},{20,16},{24,28},{28,24},{1,5},{5... | collective-permute-start | bytes 1548296 | tf_op jit(solution)/shard_map/ppermute | solution.py:234
  38.2 20.6 %collective-permute-start.8 = (bf16[144,1792]{1,0:T(8,128)(2,1)}, bf16[144,1792]{1,0:T(8,128)(2,1)S(1)}, u32[]{:S(2)}, u32[]{:S(2)}) collective-permute-start(bf16[144,1792]{1,0:T(8,128)(2,1)} %copy-done.8), channel_id=1, source_target_pairs={{0,4},{4,0},{8,12},{12,8},{16,20},{20,16},{24,28},{28,24},{1,5},{5... | collective-permute-start | bytes 1548296 | tf_op jit(solution)/shard_map/ppermute | solution.py:234
  39.5 19.4 %collective-permute-start.7 = (bf16[144,1792]{1,0:T(8,128)(2,1)}, bf16[144,1792]{1,0:T(8,128)(2,1)S(1)}, u32[]{:S(2)}, u32[]{:S(2)}) collective-permute-start(bf16[144,1792]{1,0:T(8,128)(2,1)} %copy-done.8), channel_id=1, source_target_pairs={{0,8},{4,12},{8,16},{12,20},{16,24},{20,28},{24,0},{28,4},{1,9},{5... | collective-permute-start | bytes 1548296 | tf_op jit(solution)/shard_map/ppermute | solution.py:237
  40.1 18.7 %collective-permute-start.9 = (bf16[192,1792]{1,0:T(8,128)(2,1)S(1)}, bf16[192,1792]{1,0:T(8,128)(2,1)S(1)}, u32[]{:S(2)}, u32[]{:S(2)}) collective-permute-start(bf16[192,1792]{1,0:T(8,128)(2,1)S(1)} %get-tuple-element.73.refs_4_), channel_id=1, source_target_pairs={{0,2},{1,3},{2,0},{3,1},{4,6},{5,7},{6,4},{7,5},{8,10},{9,11},{10,... | collective-permute-start | bytes 2064392 | tf_op jit(solution)/shard_map/ppermute | solution.py:243
  59.6 20.3 %collective-permute-start.10 = (bf16[144,1792]{1,0:T(8,128)(2,1)S(1)}, bf16[144,1792]{1,0:T(8,128)(2,1)S(1)}, u32[]{:S(2)}, u32[]{:S(2)}) collective-permute-start(bf16[144,1792]{1,0:T(8,128)(2,1)S(1)} %get-tuple-element.75), channel_id=1, source_target_pairs={{0,4},{4,0},{8,12},{12,8},{16,20},{20,16},{24,28},{28,24},{1,5},{5... | collective-permute-start | bytes 1548296 | tf_op jit(solution)/shard_map/ppermute | solution.py:234
  60.7 19.3 %collective-permute-start.11 = (bf16[192,1792]{1,0:T(8,128)(2,1)S(1)}, bf16[192,1792]{1,0:T(8,128)(2,1)S(1)}, u32[]{:S(2)}, u32[]{:S(2)}) collective-permute-start(bf16[192,1792]{1,0:T(8,128)(2,1)S(1)} %get-tuple-element.76.refs_3_), channel_id=1, source_target_pairs={{0,2},{1,3},{2,0},{3,1},{4,6},{5,7},{6,4},{7,5},{8,10},{9,11},{10,... | collective-permute-start | bytes 2064392 | tf_op jit(solution)/shard_map/ppermute | solution.py:243
  62.2 17.8 %collective-permute-start.6 = (bf16[192,3584]{1,0:T(8,128)(2,1)S(1)}, bf16[192,3584]{1,0:T(8,128)(2,1)S(1)}, u32[]{:S(2)}, u32[]{:S(2)}) collective-permute-start(bf16[192,3584]{1,0:T(8,128)(2,1)S(1)} %get-tuple-element.71), channel_id=1, source_target_pairs={{0,1},{1,0},{2,3},{3,2},{4,5},{5,4},{6,7},{7,6},{8,9},{9,8},{10,11... | collective-permute-start | bytes 4128776 | tf_op jit(solution)/shard_map/ppermute | solution.py:240
  80.9 11.2 %collective-permute-start.14 = (bf16[192,3584]{1,0:T(8,128)(2,1)S(1)}, bf16[192,3584]{1,0:T(8,128)(2,1)S(1)}, u32[]{:S(2)}, u32[]{:S(2)}) collective-permute-start(bf16[192,3584]{1,0:T(8,128)(2,1)S(1)} %get-tuple-element.83), channel_id=1, source_target_pairs={{0,1},{1,0},{2,3},{3,2},{4,5},{5,4},{6,7},{7,6},{8,9},{9,8},{10,11... | collective-permute-start | bytes 4128776 | tf_op jit(solution)/shard_map/ppermute | solution.py:240
  81.3 17.5 %collective-permute-start.13 = (bf16[192,1792]{1,0:T(8,128)(2,1)S(1)}, bf16[192,1792]{1,0:T(8,128)(2,1)S(1)}, u32[]{:S(2)}, u32[]{:S(2)}) collective-permute-start(bf16[192,1792]{1,0:T(8,128)(2,1)S(1)} %get-tuple-element.81.refs_0_), channel_id=1, source_target_pairs={{0,2},{1,3},{2,0},{3,1},{4,6},{5,7},{6,4},{7,5},{8,10},{9,11},{10,... | collective-permute-start | bytes 2064392 | tf_op jit(solution)/shard_map/ppermute | solution.py:243
  98.9 17.9 %collective-permute-start.19 = (bf16[192,1792]{1,0:T(8,128)(2,1)S(1)}, bf16[192,1792]{1,0:T(8,128)(2,1)S(1)}, u32[]{:S(2)}, u32[]{:S(2)}) collective-permute-start(bf16[192,1792]{1,0:T(8,128)(2,1)S(1)} %get-tuple-element.97), channel_id=1, source_target_pairs={{0,2},{1,3},{2,0},{3,1},{4,6},{5,7},{6,4},{7,5},{8,10},{9,11},{10,... | collective-permute-start | bytes 2064392 | tf_op jit(solution)/shard_map/ppermute | solution.py:243
  110.2 21.5 %collective-permute-start.18 = (bf16[192,3584]{1,0:T(8,128)(2,1)S(1)}, bf16[192,3584]{1,0:T(8,128)(2,1)S(1)}, u32[]{:S(2)}, u32[]{:S(2)}) collective-permute-start(bf16[192,3584]{1,0:T(8,128)(2,1)S(1)} %get-tuple-element.94), channel_id=1, source_target_pairs={{0,1},{1,0},{2,3},{3,2},{4,5},{5,4},{6,7},{7,6},{8,9},{9,8},{10,11... | collective-permute-start | bytes 4128776 | tf_op jit(solution)/shard_map/ppermute | solution.py:240
  117.8 12.1 %collective-permute-start.26 = (bf16[128,1792]{1,0:T(8,128)(2,1)S(1)}, bf16[128,1792]{1,0:T(8,128)(2,1)S(1)}, u32[]{:S(2)}, u32[]{:S(2)}) collective-permute-start(bf16[128,1792]{1,0:T(8,128)(2,1)S(1)} %get-tuple-element.118), channel_id=1, source_target_pairs={{0,4},{4,0},{8,12},{12,8},{16,20},{20,16},{24,28},{28,24},{1,5},{5... | collective-permute-start | bytes 1376264 | tf_op jit(solution)/shard_map/ppermute | solution.py:234
  118.8 16.7 %collective-permute-start.21 = (bf16[192,1792]{1,0:T(8,128)(2,1)S(1)}, bf16[192,1792]{1,0:T(8,128)(2,1)S(1)}, u32[]{:S(2)}, u32[]{:S(2)}) collective-permute-start(bf16[192,1792]{1,0:T(8,128)(2,1)S(1)} %get-tuple-element.104), channel_id=1, source_target_pairs={{0,2},{1,3},{2,0},{3,1},{4,6},{5,7},{6,4},{7,5},{8,10},{9,11},{10,... | collective-permute-start | bytes 2064392 | tf_op jit(solution)/shard_map/ppermute | solution.py:243
  130.0 13.0 %collective-permute-start.27 = (bf16[128,1792]{1,0:T(8,128)(2,1)S(1)}, bf16[128,1792]{1,0:T(8,128)(2,1)S(1)}, u32[]{:S(2)}, u32[]{:S(2)}) collective-permute-start(bf16[128,1792]{1,0:T(8,128)(2,1)S(1)} %add_convert_fusion.3), channel_id=1, source_target_pairs={{0,8},{4,12},{8,16},{12,20},{16,24},{20,28},{24,0},{28,4},{1,9},{5... | collective-permute-start | bytes 1376264 | tf_op jit(solution)/shard_map/ppermute | solution.py:237
  136.5 10.9 %collective-permute-start.25 = (bf16[128,1792]{1,0:T(8,128)(2,1)S(1)}, bf16[128,1792]{1,0:T(8,128)(2,1)S(1)}, u32[]{:S(2)}, u32[]{:S(2)}) collective-permute-start(bf16[128,1792]{1,0:T(8,128)(2,1)S(1)} %get-tuple-element.116), channel_id=1, source_target_pairs={{0,4},{4,0},{8,12},{12,8},{16,20},{20,16},{24,28},{28,24},{1,5},{5... | collective-permute-start | bytes 1376264 | tf_op jit(solution)/shard_map/ppermute | solution.py:234
  137.7 15.5 %collective-permute-start.20 = (bf16[192,1792]{1,0:T(8,128)(2,1)S(1)}, bf16[192,1792]{1,0:T(8,128)(2,1)S(1)}, u32[]{:S(2)}, u32[]{:S(2)}) collective-permute-start(bf16[192,1792]{1,0:T(8,128)(2,1)S(1)} %get-tuple-element.101), channel_id=1, source_target_pairs={{0,2},{1,3},{2,0},{3,1},{4,6},{5,7},{6,4},{7,5},{8,10},{9,11},{10,... | collective-permute-start | bytes 2064392 | tf_op jit(solution)/shard_map/ppermute | solution.py:243
  147.6 11.8 %collective-permute-start.28 = (bf16[128,1792]{1,0:T(8,128)(2,1)S(1)}, bf16[128,1792]{1,0:T(8,128)(2,1)S(1)}, u32[]{:S(2)}, u32[]{:S(2)}) collective-permute-start(bf16[128,1792]{1,0:T(8,128)(2,1)S(1)} %add_convert_fusion.2), channel_id=1, source_target_pairs={{0,8},{4,12},{8,16},{12,20},{16,24},{20,28},{24,0},{28,4},{1,9},{5... | collective-permute-start | bytes 1376264 | tf_op jit(solution)/shard_map/ppermute | solution.py:237
  154.2 9.7 %collective-permute-start.24 = (bf16[128,1792]{1,0:T(8,128)(2,1)S(1)}, bf16[128,1792]{1,0:T(8,128)(2,1)S(1)}, u32[]{:S(2)}, u32[]{:S(2)}) collective-permute-start(bf16[128,1792]{1,0:T(8,128)(2,1)S(1)} %get-tuple-element.114), channel_id=1, source_target_pairs={{0,4},{4,0},{8,12},{12,8},{16,20},{20,16},{24,28},{28,24},{1,5},{5... | collective-permute-start | bytes 1376264 | tf_op jit(solution)/shard_map/ppermute | solution.py:234
  155.5 14.4 %collective-permute-start.22 = (bf16[192,1792]{1,0:T(8,128)(2,1)S(1)}, bf16[192,1792]{1,0:T(8,128)(2,1)S(1)}, u32[]{:S(2)}, u32[]{:S(2)}) collective-permute-start(bf16[192,1792]{1,0:T(8,128)(2,1)S(1)} %get-tuple-element.109), channel_id=1, source_target_pairs={{0,2},{1,3},{2,0},{3,1},{4,6},{5,7},{6,4},{7,5},{8,10},{9,11},{10,... | collective-permute-start | bytes 2064392 | tf_op jit(solution)/shard_map/ppermute | solution.py:243
  164.1 10.6 %collective-permute-start.29 = (bf16[128,1792]{1,0:T(8,128)(2,1)S(1)}, bf16[128,1792]{1,0:T(8,128)(2,1)S(1)}, u32[]{:S(2)}, u32[]{:S(2)}) collective-permute-start(bf16[128,1792]{1,0:T(8,128)(2,1)S(1)} %add_convert_fusion.1), channel_id=1, source_target_pairs={{0,8},{4,12},{8,16},{12,20},{16,24},{20,28},{24,0},{28,4},{1,9},{5... | collective-permute-start | bytes 1376264 | tf_op jit(solution)/shard_map/ppermute | solution.py:237
  (18 other events, 61.0 us)

commit v5 on v4

--- a/solution.py
+++ b/solution.py
@@ -10,8 +10,8 @@
 BF = jnp.bfloat16
 F32 = jnp.float32
 TOKEN = jax.ShapeDtypeStruct((8, 128), F32)
-PACK, EXPERT, PAIR, SPREAD, LABEL = 10, 40, 2, 20, 1
-VMEM_MIB, EXPERT_MIB = 12, 22
+PACK, EXPERT, PAIR, SPREAD, LABEL = 10, 40, 2, 40, 1
+VMEM_MIB, STREAM_MIB, LAST_MIB = 12, 50, 36
 
 
 def behind(kernel, reads, after):
@@ -194,7 +194,7 @@
     pl.when(k >= both + half)(functools.partial(second, keep))
 
 
-def expert(order, near, far, feats, w_gate, w_up, w_down, after):
+def expert(order, near, far, feats, w_gate, w_up, w_down, after, mib):
     rows, width = near.shape
     units = w_gate.shape[2]
     half = width // feats
@@ -217,7 +217,7 @@
         behind(functools.partial(expert_kernel, half), 6, len(after)),
         grid_spec=grid,
         out_shape=[jax.ShapeDtypeStruct((rows, width), BF)] * 2 + [TOKEN],
-        compiler_params=pltpu.CompilerParams(vmem_limit_bytes=EXPERT_MIB * 2**20),
+        compiler_params=pltpu.CompilerParams(vmem_limit_bytes=mib * 2**20),
         cost_estimate=hint(EXPERT),
     )(order, near, far, w_gate, w_up, w_down, *after)
 
@@ -268,7 +268,7 @@
             a, token = join(pieces[t], [token])
             near[t] = a, over_core(a)
         elif step == "expert":
-            give, kept[t], token = expert(order, *near[t], feats, w_gate, w_up, w_down, [token])
+            give, kept[t], token = expert(order, *near[t], feats, w_gate, w_up, w_down, [token], STREAM_MIB if t < planes - 1 else LAST_MIB)
             given[t] = over_core(give)
         elif step == "pair":
             (own[t], *sums), token = pair_sum(kept[t], given[t], feats, [token])

time: 181 us -> 177 us (0.978)
  Pallas kernels: 40 us -> 61.3 us
  local copies, waits for them, and re-layouts: 21.8 us -> 5.88 us
  waiting for transfers between devices: 86.6 us -> 76 us
  starting transfers between devices: 30.3 us -> 32.2 us
    pallas_call x4, Pallas kernels: 32 us -> 53.2 us  [expert(): pl.pallas_call(behind(functools.partial(expert_kernel, half), 6, len(afte...]
    unnamed x24 -> x28, local copies, waits for them, and re-layouts: 21.7 us -> 5.79 us
    ppermute x8, waiting for transfers between devices: 25.7 us -> 16.4 us  [over_x(): lax.ppermute(a, 'inner', [(j, (j + 2 * s) % inners) for j in range(inners)])]
  transfers between devices with their start and end apart: 30 -> 30, of which waited for: 18 -> 20; matrix products, arithmetic and copies ran while one was open for 0% -> 0% of each run, Pallas kernels for 21% -> 33%
where the time goes in v5:
time: 177 us
  waiting for transfers between devices  76 us (43%)
  Pallas kernels  61.3 us (35%)
  starting transfers between devices  32.2 us (18%)
  local copies, waits for them, and re-layouts  5.88 us (3%)
    pallas_call x4, Pallas kernels, expert(): pl.pallas_call(behind(functools.partial(expert_kernel, half), 6, len(afte...  53.2 us
    ppermute x6, waiting for transfers between devices, over_z(): lax.ppermute(a, 'group', [(j, (j + 2) % groups) for j in range(groups)])  31.8 us
    ppermute x8, waiting for transfers between devices, over_y(): return lax.ppermute(a, 'group', [(j, j ^ 1) for j in range(groups)])  23.3 us
    ppermute x8, waiting for transfers between devices, over_x(): lax.ppermute(a, 'inner', [(j, (j + 2 * s) % inners) for j in range(inners)])  16.4 us
    ppermute x8, starting transfers between devices, over_x(): lax.ppermute(a, 'inner', [(j, (j + 2 * s) % inners) for j in range(inners)])  12 us
    ppermute x6, starting transfers between devices, over_z(): lax.ppermute(a, 'group', [(j, (j + 2) % groups) for j in range(groups)])  9.42 us
    ppermute x8, starting transfers between devices, over_y(): return lax.ppermute(a, 'group', [(j, j ^ 1) for j in range(groups)])  9.23 us
    pallas_call x14, Pallas kernels, call(): pl.pallas_call(behind(kernel, len(operands), len(after)), in_specs=[s or...  8.05 us
  transfers between devices with their start and end apart: 30, of which 20 were waited for; matrix products, arithmetic and copies ran while one was open for 0% of the time, Pallas kernels for 33%

profile of v5, /device:TPU:0, one launch (start us, length us, event | category | flops | bytes accessed | tf_op | source)
XLA Modules:
  0.0 177.0 jit_solution(5811314727100951633)
XLA Ops:
  2.4 3.1 %collective-permute-start.1 = (bf16[144,1792]{1,0:T(8,128)(2,1)S(1)}, bf16[144,1792]{1,0:T(8,128)(2,1)S(1)}, u32[]{:S(2)}, u32[]{:S(2)}) collective-permute-start(bf16[144,1792]{1,0:T(8,128)(2,1)S(1)} %get-tuple-element.62.refs_1_), channel_id=1, source_target_pairs={{0,8},{4,12},{8,16},{12,20},{16,24},{20,28},{24,0},{28,4},{1,9},{5... | collective-permute-start | bytes 1548296 | tf_op jit(solution)/shard_map/ppermute | solution.py:237
  7.0 12.3 %collective-permute-done.1.refs_3_.refs_1_ = bf16[144,1792]{1,0:T(8,128)(2,1)S(1)} collective-permute-done((bf16[144,1792]{1,0:T(8,128)(2,1)S(1)}, bf16[144,1792]{1,0:T(8,128)(2,1)S(1)}, u32[]{:S(2)}, u32[]{:S(2)}) %collective-permute-start.1) | collective-permute-done | bytes 516128 | tf_op jit(solution)/shard_map/ppermute | solution.py:237
  24.0 11.8 %collective-permute-done.3.refs_3_.refs_1_ = bf16[144,1792]{1,0:T(8,128)(2,1)S(1)} collective-permute-done((bf16[144,1792]{1,0:T(8,128)(2,1)S(1)}, bf16[144,1792]{1,0:T(8,128)(2,1)S(1)}, u32[]{:S(2)}, u32[]{:S(2)}) %collective-permute-start.3) | collective-permute-done | bytes 516128 | tf_op jit(solution)/shard_map/ppermute | solution.py:237
  42.0 13.8 %shard_map.67 = (bf16[192,3584]{1,0:T(8,128)(2,1)S(1)}, bf16[192,3584]{1,0:T(8,128)(2,1)S(1)}, f32[8,128]{1,0:T(8,128)S(1)}) custom-call(s32[8]{0:T(128)S(1)} %stack.29.refs_0_, bf16[192,3584]{1,0:T(8,128)(2,1)} %copy-done, bf16[192,3584]{1,0:T(8,128)(2,1)} %collective-permute-done.5.refs_2_, bf16[1,7168,512]{2,1,0:T(8,128)(2,1)} %refs_3_.7, ...), custom_call_target="tpu_custom_call" | custom-call | flops 40000000000 | bytes 1024 | tf_op jit(solution)/shard_map/pallas_call | solution.py:216
  55.8 1.9 %collective-permute-done.9.refs_5_ = bf16[192,1792]{1,0:T(8,128)(2,1)S(1)} collective-permute-done((bf16[192,1792]{1,0:T(8,128)(2,1)S(1)}, bf16[192,1792]{1,0:T(8,128)(2,1)S(1)}, u32[]{:S(2)}, u32[]{:S(2)}) %collective-permute-start.9) | collective-permute-done | bytes 688160 | tf_op jit(solution)/shard_map/ppermute | solution.py:243
  62.7 13.7 %shard_map.69 = (bf16[192,3584]{1,0:T(8,128)(2,1)S(1)}, bf16[192,3584]{1,0:T(8,128)(2,1)S(1)}, f32[8,128]{1,0:T(8,128)S(1)}) custom-call(s32[8]{0:T(128)S(1)} %stack.29.refs_0_, bf16[192,3584]{1,0:T(8,128)(2,1)} %copy-done.1, bf16[192,3584]{1,0:T(8,128)(2,1)} %copy-done.10, bf16[1,7168,512]{2,1,0:T(8,128)(2,1)} %refs_3_.7, bf16[1,7168,512]{2,1,0:T(8,128)(2,1)} %refs_4_.7, ...), custom_call_target="tpu_custom_call" | custom-call | flops 40000000000 | bytes 1024 | tf_op jit(solution)/shard_map/pallas_call | solution.py:216
  81.6 13.8 %shard_map.71 = (bf16[192,3584]{1,0:T(8,128)(2,1)S(1)}, bf16[192,3584]{1,0:T(8,128)(2,1)S(1)}, f32[8,128]{1,0:T(8,128)S(1)}) custom-call(s32[8]{0:T(128)S(1)} %stack.29.refs_0_, bf16[192,3584]{1,0:T(8,128)(2,1)} %copy-done.2, bf16[192,3584]{1,0:T(8,128)(2,1)} %copy-done.11, bf16[1,7168,512]{2,1,0:T(8,128)(2,1)} %refs_3_.7, bf16[1,7168,512]{2,1,0:T(8,128)(2,1)} %refs_4_.7, ...), custom_call_target="tpu_custom_call" | custom-call | flops 40000000000 | bytes 1024 | tf_op jit(solution)/shard_map/pallas_call | solution.py:216
  98.8 1.7 collective-permute-done.16.refs_2_
  100.5 12.0 %shard_map.75 = (bf16[192,3584]{1,0:T(8,128)(2,1)S(1)}, bf16[192,3584]{1,0:T(8,128)(2,1)S(1)}, f32[8,128]{1,0:T(8,128)S(1)}) custom-call(s32[8]{0:T(128)S(1)} %stack.29.refs_0_, bf16[192,3584]{1,0:T(8,128)(2,1)S(1)} %get-tuple-element.88.refs_1_, bf16[192,3584]{1,0:T(8,128)(2,1)S(1)} %collective-permute-done.16.refs_2_, bf16[1,7168,512]{2,1,0:T(8,128)(2,1)S(1)} %bitcast.10, ...), custom_call_target="tpu_custom_call" | custom-call | flops 40000000000 | bytes 1024 | tf_op jit(solution)/shard_map/pallas_call | solution.py:216
  114.9 1.6 collective-permute-start.26
  118.0 8.7 %collective-permute-done.26 = bf16[128,1792]{1,0:T(8,128)(2,1)S(1)} collective-permute-done((bf16[128,1792]{1,0:T(8,128)(2,1)S(1)}, bf16[128,1792]{1,0:T(8,128)(2,1)S(1)}, u32[]{:S(2)}, u32[]{:S(2)}) %collective-permute-start.26) | collective-permute-done | bytes 458784 | tf_op jit(solution)/shard_map/ppermute | solution.py:234
  126.8 1.6 collective-permute-start.27
  128.7 4.1 %collective-permute-done.21.refs_3_ = bf16[192,1792]{1,0:T(8,128)(2,1)S(1)} collective-permute-done((bf16[192,1792]{1,0:T(8,128)(2,1)S(1)}, bf16[192,1792]{1,0:T(8,128)(2,1)S(1)}, u32[]{:S(2)}, u32[]{:S(2)}) %collective-permute-start.21) | collective-permute-done | bytes 688160 | tf_op jit(solution)/shard_map/ppermute | solution.py:243
  135.9 3.5 %collective-permute-done.27 = bf16[128,1792]{1,0:T(8,128)(2,1)S(1)} collective-permute-done((bf16[128,1792]{1,0:T(8,128)(2,1)S(1)}, bf16[128,1792]{1,0:T(8,128)(2,1)S(1)}, u32[]{:S(2)}, u32[]{:S(2)}) %collective-permute-start.27) | collective-permute-done | bytes 458784 | tf_op jit(solution)/shard_map/ppermute | solution.py:237
  139.4 5.0 %collective-permute-done.25 = bf16[128,1792]{1,0:T(8,128)(2,1)S(1)} collective-permute-done((bf16[128,1792]{1,0:T(8,128)(2,1)S(1)}, bf16[128,1792]{1,0:T(8,128)(2,1)S(1)}, u32[]{:S(2)}, u32[]{:S(2)}) %collective-permute-start.25) | collective-permute-done | bytes 458784 | tf_op jit(solution)/shard_map/ppermute | solution.py:234
  144.6 1.7 collective-permute-start.28
  146.2 3.4 %collective-permute-done.20.refs_3_ = bf16[192,1792]{1,0:T(8,128)(2,1)S(1)} collective-permute-done((bf16[192,1792]{1,0:T(8,128)(2,1)S(1)}, bf16[192,1792]{1,0:T(8,128)(2,1)S(1)}, u32[]{:S(2)}, u32[]{:S(2)}) %collective-permute-start.20) | collective-permute-done | bytes 688160 | tf_op jit(solution)/shard_map/ppermute | solution.py:243
  152.5 1.6 collective-permute-start.22
  154.1 1.9 %collective-permute-done.28 = bf16[128,1792]{1,0:T(8,128)(2,1)S(1)} collective-permute-done((bf16[128,1792]{1,0:T(8,128)(2,1)S(1)}, bf16[128,1792]{1,0:T(8,128)(2,1)S(1)}, u32[]{:S(2)}, u32[]{:S(2)}) %collective-permute-start.28) | collective-permute-done | bytes 458784 | tf_op jit(solution)/shard_map/ppermute | solution.py:237
  156.0 4.0 %collective-permute-done.24 = bf16[128,1792]{1,0:T(8,128)(2,1)S(1)} collective-permute-done((bf16[128,1792]{1,0:T(8,128)(2,1)S(1)}, bf16[128,1792]{1,0:T(8,128)(2,1)S(1)}, u32[]{:S(2)}, u32[]{:S(2)}) %collective-permute-start.24) | collective-permute-done | bytes 458784 | tf_op jit(solution)/shard_map/ppermute | solution.py:234
  160.1 1.6 collective-permute-start.29
  161.8 4.7 %collective-permute-done.22.refs_3_ = bf16[192,1792]{1,0:T(8,128)(2,1)S(1)} collective-permute-done((bf16[192,1792]{1,0:T(8,128)(2,1)S(1)}, bf16[192,1792]{1,0:T(8,128)(2,1)S(1)}, u32[]{:S(2)}, u32[]{:S(2)}) %collective-permute-start.22) | collective-permute-done | bytes 688160 | tf_op jit(solution)/shard_map/ppermute | solution.py:243
  168.2 2.3 %collective-permute-done.29 = bf16[128,1792]{1,0:T(8,128)(2,1)S(1)} collective-permute-done((bf16[128,1792]{1,0:T(8,128)(2,1)S(1)}, bf16[128,1792]{1,0:T(8,128)(2,1)S(1)}, u32[]{:S(2)}, u32[]{:S(2)}) %collective-permute-start.29) | collective-permute-done | bytes 458784 | tf_op jit(solution)/shard_map/ppermute | solution.py:237
  170.5 5.6 %collective-permute-done.23 = bf16[128,1792]{1,0:T(8,128)(2,1)S(1)} collective-permute-done((bf16[128,1792]{1,0:T(8,128)(2,1)S(1)}, bf16[128,1792]{1,0:T(8,128)(2,1)S(1)}, u32[]{:S(2)}, u32[]{:S(2)}) %collective-permute-start.23) | collective-permute-done | bytes 458784 | tf_op jit(solution)/shard_map/ppermute | solution.py:234
  (88 shorter events, 41.3 us)
Async XLA Ops:
  2.4 16.8 %collective-permute-start.1 = (bf16[144,1792]{1,0:T(8,128)(2,1)S(1)}, bf16[144,1792]{1,0:T(8,128)(2,1)S(1)}, u32[]{:S(2)}, u32[]{:S(2)}) collective-permute-start(bf16[144,1792]{1,0:T(8,128)(2,1)S(1)} %get-tuple-element.62.refs_1_), channel_id=1, source_target_pairs={{0,8},{4,12},{8,16},{12,20},{16,24},{20,28},{24,0},{28,4},{1,9},{5... | collective-permute-start | bytes 1548296 | tf_op jit(solution)/shard_map/ppermute | solution.py:237
  5.5 13.8 %collective-permute-start = (bf16[144,1792]{1,0:T(8,128)(2,1)S(1)}, bf16[144,1792]{1,0:T(8,128)(2,1)S(1)}, u32[]{:S(2)}, u32[]{:S(2)}) collective-permute-start(bf16[144,1792]{1,0:T(8,128)(2,1)S(1)} %get-tuple-element.62.refs_1_), channel_id=1, source_target_pairs={{0,4},{4,0},{8,12},{12,8},{16,20},{20,16},{24,28},{28,24},{1,5},{5... | collective-permute-start | bytes 1548296 | tf_op jit(solution)/shard_map/ppermute | solution.py:234
  20.1 16.6 %collective-permute-start.4 = (bf16[192,1792]{1,0:T(8,128)(2,1)S(1)}, bf16[192,1792]{1,0:T(8,128)(2,1)S(1)}, u32[]{:S(2)}, u32[]{:S(2)}) collective-permute-start(bf16[192,1792]{1,0:T(8,128)(2,1)S(1)} %get-tuple-element.66.refs_4_), channel_id=1, source_target_pairs={{0,2},{1,3},{2,0},{3,1},{4,6},{5,7},{6,4},{7,5},{8,10},{9,11},{10,... | collective-permute-start | bytes 2064392 | tf_op jit(solution)/shard_map/ppermute | solution.py:243
  21.6 14.2 %collective-permute-start.3 = (bf16[144,1792]{1,0:T(8,128)(2,1)S(1)}, bf16[144,1792]{1,0:T(8,128)(2,1)S(1)}, u32[]{:S(2)}, u32[]{:S(2)}) collective-permute-start(bf16[144,1792]{1,0:T(8,128)(2,1)S(1)} %get-tuple-element.65), channel_id=1, source_target_pairs={{0,8},{4,12},{8,16},{12,20},{16,24},{20,28},{24,0},{28,4},{1,9},{5... | collective-permute-start | bytes 1548296 | tf_op jit(solution)/shard_map/ppermute | solution.py:237
  22.5 13.3 %collective-permute-start.2 = (bf16[144,1792]{1,0:T(8,128)(2,1)S(1)}, bf16[144,1792]{1,0:T(8,128)(2,1)S(1)}, u32[]{:S(2)}, u32[]{:S(2)}) collective-permute-start(bf16[144,1792]{1,0:T(8,128)(2,1)S(1)} %get-tuple-element.65), channel_id=1, source_target_pairs={{0,4},{4,0},{8,12},{12,8},{16,20},{20,16},{24,28},{28,24},{1,5},{5... | collective-permute-start | bytes 1548296 | tf_op jit(solution)/shard_map/ppermute | solution.py:234
  38.7 17.1 %collective-permute-start.8 = (bf16[144,1792]{1,0:T(8,128)(2,1)S(1)}, bf16[144,1792]{1,0:T(8,128)(2,1)S(1)}, u32[]{:S(2)}, u32[]{:S(2)}) collective-permute-start(bf16[144,1792]{1,0:T(8,128)(2,1)S(1)} %get-tuple-element.72), channel_id=1, source_target_pairs={{0,4},{4,0},{8,12},{12,8},{16,20},{20,16},{24,28},{28,24},{1,5},{5... | collective-permute-start | bytes 1548296 | tf_op jit(solution)/shard_map/ppermute | solution.py:234
  40.0 15.8 %collective-permute-start.7 = (bf16[144,1792]{1,0:T(8,128)(2,1)S(1)}, bf16[144,1792]{1,0:T(8,128)(2,1)S(1)}, u32[]{:S(2)}, u32[]{:S(2)}) collective-permute-start(bf16[144,1792]{1,0:T(8,128)(2,1)S(1)} %get-tuple-element.72), channel_id=1, source_target_pairs={{0,8},{4,12},{8,16},{12,20},{16,24},{20,28},{24,0},{28,4},{1,9},{5... | collective-permute-start | bytes 1548296 | tf_op jit(solution)/shard_map/ppermute | solution.py:237
  40.5 17.2 %collective-permute-start.9 = (bf16[192,1792]{1,0:T(8,128)(2,1)S(1)}, bf16[192,1792]{1,0:T(8,128)(2,1)S(1)}, u32[]{:S(2)}, u32[]{:S(2)}) collective-permute-start(bf16[192,1792]{1,0:T(8,128)(2,1)S(1)} %get-tuple-element.73.refs_4_), channel_id=1, source_target_pairs={{0,2},{1,3},{2,0},{3,1},{4,6},{5,7},{6,4},{7,5},{8,10},{9,11},{10,... | collective-permute-start | bytes 2064392 | tf_op jit(solution)/shard_map/ppermute | solution.py:243
  58.5 18.0 %collective-permute-start.10 = (bf16[144,1792]{1,0:T(8,128)(2,1)S(1)}, bf16[144,1792]{1,0:T(8,128)(2,1)S(1)}, u32[]{:S(2)}, u32[]{:S(2)}) collective-permute-start(bf16[144,1792]{1,0:T(8,128)(2,1)S(1)} %get-tuple-element.75), channel_id=1, source_target_pairs={{0,4},{4,0},{8,12},{12,8},{16,20},{20,16},{24,28},{28,24},{1,5},{5... | collective-permute-start | bytes 1548296 | tf_op jit(solution)/shard_map/ppermute | solution.py:234
  59.1 17.5 %collective-permute-start.11 = (bf16[192,1792]{1,0:T(8,128)(2,1)S(1)}, bf16[192,1792]{1,0:T(8,128)(2,1)S(1)}, u32[]{:S(2)}, u32[]{:S(2)}) collective-permute-start(bf16[192,1792]{1,0:T(8,128)(2,1)S(1)} %get-tuple-element.76.refs_3_), channel_id=1, source_target_pairs={{0,2},{1,3},{2,0},{3,1},{4,6},{5,7},{6,4},{7,5},{8,10},{9,11},{10,... | collective-permute-start | bytes 2064392 | tf_op jit(solution)/shard_map/ppermute | solution.py:243
  60.6 16.0 %collective-permute-start.6 = (bf16[192,3584]{1,0:T(8,128)(2,1)S(1)}, bf16[192,3584]{1,0:T(8,128)(2,1)S(1)}, u32[]{:S(2)}, u32[]{:S(2)}) collective-permute-start(bf16[192,3584]{1,0:T(8,128)(2,1)S(1)} %get-tuple-element.71), channel_id=1, source_target_pairs={{0,1},{1,0},{2,3},{3,2},{4,5},{5,4},{6,7},{7,6},{8,9},{9,8},{10,11... | collective-permute-start | bytes 4128776 | tf_op jit(solution)/shard_map/ppermute | solution.py:240
  77.4 18.1 %collective-permute-start.14 = (bf16[192,3584]{1,0:T(8,128)(2,1)S(1)}, bf16[192,3584]{1,0:T(8,128)(2,1)S(1)}, u32[]{:S(2)}, u32[]{:S(2)}) collective-permute-start(bf16[192,3584]{1,0:T(8,128)(2,1)S(1)} %get-tuple-element.83), channel_id=1, source_target_pairs={{0,1},{1,0},{2,3},{3,2},{4,5},{5,4},{6,7},{7,6},{8,9},{9,8},{10,11... | collective-permute-start | bytes 4128776 | tf_op jit(solution)/shard_map/ppermute | solution.py:240
  77.9 18.0 %collective-permute-start.13 = (bf16[192,1792]{1,0:T(8,128)(2,1)S(1)}, bf16[192,1792]{1,0:T(8,128)(2,1)S(1)}, u32[]{:S(2)}, u32[]{:S(2)}) collective-permute-start(bf16[192,1792]{1,0:T(8,128)(2,1)S(1)} %get-tuple-element.81.refs_0_), channel_id=1, source_target_pairs={{0,2},{1,3},{2,0},{3,1},{4,6},{5,7},{6,4},{7,5},{8,10},{9,11},{10,... | collective-permute-start | bytes 2064392 | tf_op jit(solution)/shard_map/ppermute | solution.py:243
  96.4 17.5 %collective-permute-start.19 = (bf16[192,1792]{1,0:T(8,128)(2,1)S(1)}, bf16[192,1792]{1,0:T(8,128)(2,1)S(1)}, u32[]{:S(2)}, u32[]{:S(2)}) collective-permute-start(bf16[192,1792]{1,0:T(8,128)(2,1)S(1)} %get-tuple-element.97), channel_id=1, source_target_pairs={{0,2},{1,3},{2,0},{3,1},{4,6},{5,7},{6,4},{7,5},{8,10},{9,11},{10,... | collective-permute-start | bytes 2064392 | tf_op jit(solution)/shard_map/ppermute | solution.py:243
  112.5 15.9 %collective-permute-start.18 = (bf16[192,3584]{1,0:T(8,128)(2,1)S(1)}, bf16[192,3584]{1,0:T(8,128)(2,1)S(1)}, u32[]{:S(2)}, u32[]{:S(2)}) collective-permute-start(bf16[192,3584]{1,0:T(8,128)(2,1)S(1)} %get-tuple-element.94), channel_id=1, source_target_pairs={{0,1},{1,0},{2,3},{3,2},{4,5},{5,4},{6,7},{7,6},{8,9},{9,8},{10,11... | collective-permute-start | bytes 4128776 | tf_op jit(solution)/shard_map/ppermute | solution.py:240
  114.9 11.8 %collective-permute-start.26 = (bf16[128,1792]{1,0:T(8,128)(2,1)S(1)}, bf16[128,1792]{1,0:T(8,128)(2,1)S(1)}, u32[]{:S(2)}, u32[]{:S(2)}) collective-permute-start(bf16[128,1792]{1,0:T(8,128)(2,1)S(1)} %get-tuple-element.118), channel_id=1, source_target_pairs={{0,4},{4,0},{8,12},{12,8},{16,20},{20,16},{24,28},{28,24},{1,5},{5... | collective-permute-start | bytes 1376264 | tf_op jit(solution)/shard_map/ppermute | solution.py:234
  116.5 16.4 %collective-permute-start.21 = (bf16[192,1792]{1,0:T(8,128)(2,1)S(1)}, bf16[192,1792]{1,0:T(8,128)(2,1)S(1)}, u32[]{:S(2)}, u32[]{:S(2)}) collective-permute-start(bf16[192,1792]{1,0:T(8,128)(2,1)S(1)} %get-tuple-element.104), channel_id=1, source_target_pairs={{0,2},{1,3},{2,0},{3,1},{4,6},{5,7},{6,4},{7,5},{8,10},{9,11},{10,... | collective-permute-start | bytes 2064392 | tf_op jit(solution)/shard_map/ppermute | solution.py:243
  126.8 12.7 %collective-permute-start.27 = (bf16[128,1792]{1,0:T(8,128)(2,1)S(1)}, bf16[128,1792]{1,0:T(8,128)(2,1)S(1)}, u32[]{:S(2)}, u32[]{:S(2)}) collective-permute-start(bf16[128,1792]{1,0:T(8,128)(2,1)S(1)} %add_convert_fusion.3), channel_id=1, source_target_pairs={{0,8},{4,12},{8,16},{12,20},{16,24},{20,28},{24,0},{28,4},{1,9},{5... | collective-permute-start | bytes 1376264 | tf_op jit(solution)/shard_map/ppermute | solution.py:237
  133.8 10.6 %collective-permute-start.25 = (bf16[128,1792]{1,0:T(8,128)(2,1)S(1)}, bf16[128,1792]{1,0:T(8,128)(2,1)S(1)}, u32[]{:S(2)}, u32[]{:S(2)}) collective-permute-start(bf16[128,1792]{1,0:T(8,128)(2,1)S(1)} %get-tuple-element.116), channel_id=1, source_target_pairs={{0,4},{4,0},{8,12},{12,8},{16,20},{20,16},{24,28},{28,24},{1,5},{5... | collective-permute-start | bytes 1376264 | tf_op jit(solution)/shard_map/ppermute | solution.py:234
  134.4 15.2 %collective-permute-start.20 = (bf16[192,1792]{1,0:T(8,128)(2,1)S(1)}, bf16[192,1792]{1,0:T(8,128)(2,1)S(1)}, u32[]{:S(2)}, u32[]{:S(2)}) collective-permute-start(bf16[192,1792]{1,0:T(8,128)(2,1)S(1)} %get-tuple-element.101), channel_id=1, source_target_pairs={{0,2},{1,3},{2,0},{3,1},{4,6},{5,7},{6,4},{7,5},{8,10},{9,11},{10,... | collective-permute-start | bytes 2064392 | tf_op jit(solution)/shard_map/ppermute | solution.py:243
  144.6 11.4 %collective-permute-start.28 = (bf16[128,1792]{1,0:T(8,128)(2,1)S(1)}, bf16[128,1792]{1,0:T(8,128)(2,1)S(1)}, u32[]{:S(2)}, u32[]{:S(2)}) collective-permute-start(bf16[128,1792]{1,0:T(8,128)(2,1)S(1)} %add_convert_fusion.2), channel_id=1, source_target_pairs={{0,8},{4,12},{8,16},{12,20},{16,24},{20,28},{24,0},{28,4},{1,9},{5... | collective-permute-start | bytes 1376264 | tf_op jit(solution)/shard_map/ppermute | solution.py:237
  150.6 9.4 %collective-permute-start.24 = (bf16[128,1792]{1,0:T(8,128)(2,1)S(1)}, bf16[128,1792]{1,0:T(8,128)(2,1)S(1)}, u32[]{:S(2)}, u32[]{:S(2)}) collective-permute-start(bf16[128,1792]{1,0:T(8,128)(2,1)S(1)} %get-tuple-element.114), channel_id=1, source_target_pairs={{0,4},{4,0},{8,12},{12,8},{16,20},{20,16},{24,28},{28,24},{1,5},{5... | collective-permute-start | bytes 1376264 | tf_op jit(solution)/shard_map/ppermute | solution.py:234
  152.5 14.0 %collective-permute-start.22 = (bf16[192,1792]{1,0:T(8,128)(2,1)S(1)}, bf16[192,1792]{1,0:T(8,128)(2,1)S(1)}, u32[]{:S(2)}, u32[]{:S(2)}) collective-permute-start(bf16[192,1792]{1,0:T(8,128)(2,1)S(1)} %get-tuple-element.109), channel_id=1, source_target_pairs={{0,2},{1,3},{2,0},{3,1},{4,6},{5,7},{6,4},{7,5},{8,10},{9,11},{10,... | collective-permute-start | bytes 2064392 | tf_op jit(solution)/shard_map/ppermute | solution.py:243
  160.1 10.3 %collective-permute-start.29 = (bf16[128,1792]{1,0:T(8,128)(2,1)S(1)}, bf16[128,1792]{1,0:T(8,128)(2,1)S(1)}, u32[]{:S(2)}, u32[]{:S(2)}) collective-permute-start(bf16[128,1792]{1,0:T(8,128)(2,1)S(1)} %add_convert_fusion.1), channel_id=1, source_target_pairs={{0,8},{4,12},{8,16},{12,20},{16,24},{20,28},{24,0},{28,4},{1,9},{5... | collective-permute-start | bytes 1376264 | tf_op jit(solution)/shard_map/ppermute | solution.py:237
  (20 other events, 57.4 us)
